TPU v7x, 32 devices: a whole 2x2x4 slice. The times are simulated.
32 devices in a mesh: fsdp: 4 (over x, core), tp: 8 (over z, y).
Axes of the slice: x: 2, y: 2, z: 4, core: 2. Of those that a mesh axis runs over, the one named last changes fastest.
Arguments:
- inputs: bfloat16 [128, 4, 8192], P('tp', None, 'fsdp'), may hold values from -6 to 6
- featurizer: bfloat16 [8192, 3, 8192], P('fsdp', None, 'tp'), may hold values from -0.0625 to 0.0625
- short_filter: float32 [3, 3, 8192], P(None, None, 'tp'), may hold values from -3 to 3
- long_filter: float32 [512, 128], P('tp'), may hold values from -1.2 to 1.2
- decay_rate: float32 [512], P('tp'), may hold values from 0.004 to 0.08
- skip_gain: float32 [8192], P('tp'), may hold values from -1 to 1
- output_grad: bfloat16 [128, 4, 8192], P(None, 'fsdp', 'tp'), may hold values from -6 to 6
Outputs:
- hyena_out: bfloat16 [128, 4, 8192], P(None, 'fsdp', 'tp')
- input_grad: bfloat16 [128, 4, 8192], P('tp', None, 'fsdp')
- weight_grad: bfloat16 [8192, 3, 8192], P('fsdp', None, 'tp')
All inputs are finite; a program needn't handle non-finite values.
Results may differ from a plain program's by a relative error of at most 0.028.
Values may be sent and summed in bfloat16 or wider, within the bound.
A program may use at most 128 MiB of HBM per device.

v0:
```python
import jax
import jax.numpy as jnp
from jax import lax
from jax.sharding import PartitionSpec as P


def from_behind(x, axis, by):
    devices = lax.axis_size(axis)
    pairs = [(i, i + by) for i in range(devices) if 0 <= i + by < devices]
    return lax.ppermute(x, axis, pairs)


def toeplitz_pair(kernel, tokens):
    tap_count = kernel.shape[1]
    positions = jnp.arange(tokens)
    lag_grid = positions[:, None] - positions[None, :]
    near_inside = (lag_grid >= 0) & (lag_grid < tap_count)
    near_taken = jnp.take(kernel, jnp.clip(lag_grid, 0, tap_count - 1), axis=1)
    near_matrix = jnp.where(near_inside[None], near_taken, jnp.zeros_like(near_taken))
    far_grid = lag_grid + tokens
    far_inside = far_grid < tap_count
    far_taken = jnp.take(kernel, jnp.clip(far_grid, 0, tap_count - 1), axis=1)
    far_matrix = jnp.where(far_inside[None], far_taken, jnp.zeros_like(far_taken))
    return (near_matrix, far_matrix)


def add_sources(pieces):
    return tuple((jnp.sum(member, axis=1) for member in pieces))


def shards(inputs, featurizer, short_filter, long_filter, decay_rate, skip_gain, output_grad):
    gathered = lax.all_gather(inputs, "tp", axis=0, tiled=True)
    tokens, blocks, block_rows = gathered.shape
    halo_rows = short_filter.shape[0] - 1
    channels = featurizer.shape[2]
    wide_columns = 3 * channels
    border = jnp.zeros((halo_rows, 1, block_rows), gathered.dtype)
    earlier_rows = jnp.concatenate([border, gathered[tokens - halo_rows :, : blocks - 1]], axis=1)
    extended = jnp.concatenate([earlier_rows, gathered], axis=0)
    flat_ext = extended.reshape((tokens + halo_rows) * blocks, block_rows)
    partials = [
        jnp.dot(flat_ext, featurizer[:, stream, :], preferred_element_type=jnp.float32).reshape(
            tokens + halo_rows, blocks, channels
        )
        for stream in range(3)
    ]
    summed = add_sources(
        (
            lax.all_to_all(
                partials[0].astype(jnp.bfloat16), "fsdp", split_axis=1, concat_axis=1, tiled=True
            ).astype(jnp.float32),
            lax.all_to_all(
                partials[1].astype(jnp.bfloat16), "fsdp", split_axis=1, concat_axis=1, tiled=True
            ).astype(jnp.float32),
            lax.all_to_all(
                partials[2].astype(jnp.bfloat16), "fsdp", split_axis=1, concat_axis=1, tiled=True
            ).astype(jnp.float32),
        )
    )
    features = jnp.stack([member.astype(jnp.bfloat16) for member in summed], axis=1)
    feat_wide = features.astype(jnp.float32)
    filtered = short_filter[0] * feat_wide[halo_rows:]
    for lag_step in range(1, halo_rows + 1):
        filtered = (
            filtered
            + short_filter[lag_step]
            * feat_wide[halo_rows - lag_step : halo_rows - lag_step + tokens]
        )
    queries = filtered[:, 0]
    key_part = filtered[:, 1]
    value_part = filtered[:, 2]
    product = key_part * value_part
    offsets = jnp.arange(long_filter.shape[1]).astype(jnp.float32)
    kernel = long_filter * jnp.exp(-decay_rate[:, None] * offsets[None, :])
    near_matrix, far_matrix = toeplitz_pair(kernel, tokens)
    filter_count = kernel.shape[0]
    group_width = channels // filter_count
    grouped = product.reshape(tokens, filter_count, group_width)
    local_conv = jnp.einsum(
        "nst,tnc->snc", near_matrix, grouped, precision=lax.Precision.HIGHEST
    ).reshape(tokens, channels)
    earlier = from_behind(product.astype(jnp.bfloat16), "fsdp", 1).astype(product.dtype)
    far_conv = jnp.einsum(
        "nst,tnc->snc",
        far_matrix,
        earlier.reshape(tokens, filter_count, group_width),
        precision=lax.Precision.HIGHEST,
    ).reshape(tokens, channels)
    convolved = local_conv + far_conv + skip_gain * product
    hyena_out = (queries * convolved).astype(jnp.bfloat16).reshape(tokens, 1, channels)
    upstream = output_grad.reshape(tokens, channels).astype(jnp.float32)
    query_grad = upstream * convolved
    conv_grad = upstream * queries
    conv_grouped = conv_grad.reshape(tokens, filter_count, group_width)
    local_back = jnp.einsum(
        "nst,snc->tnc", near_matrix, conv_grouped, precision=lax.Precision.HIGHEST
    ).reshape(tokens, channels)
    later_grad = from_behind(conv_grad.astype(jnp.bfloat16), "fsdp", -1).astype(conv_grad.dtype)
    far_back = jnp.einsum(
        "nst,snc->tnc",
        far_matrix,
        later_grad.reshape(tokens, filter_count, group_width),
        precision=lax.Precision.HIGHEST,
    ).reshape(tokens, channels)
    product_grad = local_back + far_back + skip_gain * conv_grad
    filtered_grad = jnp.stack(
        [query_grad, product_grad * value_part, product_grad * key_part], axis=1
    )
    next_head = from_behind(filtered_grad[:halo_rows], "fsdp", -1)
    padded = jnp.concatenate([filtered_grad, next_head], axis=0)
    feature_grad = short_filter[0] * filtered_grad
    for lag_step in range(1, halo_rows + 1):
        feature_grad = feature_grad + short_filter[lag_step] * padded[lag_step : lag_step + tokens]
    grad_own = feature_grad.astype(jnp.bfloat16).reshape(tokens, 1, wide_columns)
    grad_all = lax.all_gather(grad_own, "fsdp", axis=1, tiled=True)
    weight_block = featurizer.reshape(block_rows, wide_columns)
    weight_grad = lax.dot_general(
        gathered, grad_all, (((0, 1), (0, 1)), ((), ())), preferred_element_type=jnp.float32
    )
    weight_grad = weight_grad.astype(jnp.bfloat16).reshape(featurizer.shape)
    own_count = tokens // lax.axis_size("tp")
    flat_piece = grad_all.reshape(own_count * lax.axis_size("tp") * blocks, wide_columns)
    result = lax.dot_general(
        flat_piece, weight_block, (((1,), (1,)), ((), ())), preferred_element_type=jnp.float32
    )
    input_grad = lax.psum_scatter(
        result.reshape(own_count * lax.axis_size("tp"), blocks, block_rows).astype(jnp.bfloat16),
        "tp",
        scatter_dimension=0,
        tiled=True,
    )
    return (hyena_out, input_grad, weight_grad)


def solution(mesh):
    in_specs = (
        P("tp", None, "fsdp"),
        P("fsdp", None, "tp"),
        P(None, None, "tp"),
        P("tp", None),
        P("tp"),
        P("tp"),
        P(None, "fsdp", "tp"),
    )
    out_specs = (P(None, "fsdp", "tp"), P("tp", None, "fsdp"), P("fsdp", None, "tp"))
    return jax.shard_map(shards, mesh=mesh, in_specs=in_specs, out_specs=out_specs, check_vma=False)
```

profile of v0, /device:TPU:0, one launch (start us, length us, event | category | flops | bytes accessed | tf_op | source)
XLA Modules:
  0.0 403.7 jit_solution(736225845524827256)
XLA Ops:
  7.2 0.0 all-gather.3.cloned.1.call-start
  7.2 1.8 copy.36
  9.0 0.0 all-gather.3.cloned.1.call-update
  9.0 0.8 copy.38
  9.9 0.7 neg.4
  10.6 52.2 %all-gather.3.cloned.1.call-done = bf16[128,4,2048]{2,0,1:T(8,128)(2,1)} async-done(((bf16[16,4,2048]{2,0,1:T(8,128)(2,1)}), bf16[128,4,2048]{2,0,1:T(8,128)(2,1)}) %all-gather.3.cloned.1.call-update) | async-done | bytes 2097168 | tf_op jit(solution)/shard_map/all_gather | solution.py:32
  62.8 0.9 slice.71
  63.7 6.3 %fusion.42 = bf16[130,4,1024]{2,0,1:T(8,128)(2,1)} fusion(bf16[2048,3,1024]{2,0,1:T(8,128)(2,1)} %param.10, bf16[2,3,2048]{2,0,1:T(2,128)(2,1)S(1)} %slice.71, bf16[128,4,2048]{2,0,1:T(8,128)(2,1)} %all-gather.3.cloned.1.call-done), kind=kOutput, calls=%fused_computation.52 | convolution fusion | flops 2187960320 | bytes 7380992 | tf_op jit(solution)/shard_map/dot_general | solution.py:42
  70.0 3.5 all-to-all-start.2
  73.5 6.3 %fusion.39 = bf16[130,4,1024]{2,0,1:T(8,128)(2,1)} fusion(bf16[2048,3,1024]{2,0,1:T(8,128)(2,1)} %param.10, bf16[2,3,2048]{2,0,1:T(2,128)(2,1)S(1)} %slice.71, bf16[128,4,2048]{2,0,1:T(8,128)(2,1)} %all-gather.3.cloned.1.call-done), kind=kOutput, calls=%fused_computation.51 | convolution fusion | flops 2187960320 | bytes 7380992 | tf_op jit(solution)/shard_map/dot_general | solution.py:42
  79.8 8.8 %all-to-all-done.2 = bf16[130,4,1024]{2,0,1:T(8,128)(2,1)S(1)} async-done(((bf16[130,4,1024]{2,0,1:T(8,128)(2,1)}), bf16[130,4,1024]{2,0,1:T(8,128)(2,1)S(1)}, u32[]{:S(2)}, u32[]{:S(2)}) %all-to-all-start.2) | async-done | bytes 1064992 | tf_op jit(solution)/shard_map/all_to_all | solution.py:55
  88.6 3.5 all-to-all-start.1
  92.2 0.1 exponential_multiply_fusion
  92.3 6.3 %fusion.36 = bf16[130,4,1024]{2,0,1:T(8,128)(2,1)} fusion(bf16[2048,3,1024]{2,0,1:T(8,128)(2,1)} %param.10, bf16[2,3,2048]{2,0,1:T(2,128)(2,1)S(1)} %slice.71, bf16[128,4,2048]{2,0,1:T(8,128)(2,1)} %all-gather.3.cloned.1.call-done), kind=kOutput, calls=%fused_computation.50 | convolution fusion | flops 2187960320 | bytes 7380992 | tf_op jit(solution)/shard_map/dot_general | solution.py:42
  98.6 8.7 %all-to-all-done.1 = bf16[130,4,1024]{2,0,1:T(8,128)(2,1)S(1)} async-done(((bf16[130,4,1024]{2,0,1:T(8,128)(2,1)}), bf16[130,4,1024]{2,0,1:T(8,128)(2,1)S(1)}, u32[]{:S(2)}, u32[]{:S(2)}) %all-to-all-start.1) | async-done | bytes 1064992 | tf_op jit(solution)/shard_map/all_to_all | solution.py:52
  107.3 3.5 all-to-all-start
  110.8 0.0 all-gather.5.cloned.1.call-start
  110.9 54.9 %gather_fusion = f32[16384,64]{1,0:T(8,128)} fusion(f32[64,128]{0,1:T(8,128)S(1)} %exponential_multiply_fusion, s32[16384]{0:T(1024)S(1)} %bitcast_clamp_fusion.1), kind=kCustom, calls=%fused_computation.clone | custom fusion | bytes 8454144 | tf_op jit(solution)/shard_map/jit(_take)/gather | solution.py:18
  165.8 7.4 %copy.39 = f32[128,128,64]{1,0,2:T(8,128)} copy(f32[128,128,64]{2,1,0:T(8,128)} %bitcast.77) | data formatting | bytes 8388608 | tf_op jit(solution)/shard_map/jit(_take)/gather | solution.py:18
  173.2 54.9 %gather_fusion.1 = f32[16384,64]{1,0:T(8,128)} fusion(f32[64,128]{0,1:T(8,128)S(1)} %exponential_multiply_fusion, s32[16384]{0:T(1024)S(1)} %bitcast_clamp_fusion), kind=kCustom, calls=%fused_computation.1.clone | custom fusion | bytes 8454144 | tf_op jit(solution)/shard_map/jit(_take)/gather | solution.py:22
  228.1 7.3 %copy.41 = f32[128,128,64]{1,0,2:T(8,128)} copy(f32[128,128,64]{2,1,0:T(8,128)} %bitcast.76) | data formatting | bytes 8388608 | tf_op jit(solution)/shard_map/jit(_take)/gather | solution.py:22
  235.6 1.0 reduce_sum.38
  236.5 0.2 reduce_sum.37
  236.7 0.0 all-to-all-done
  236.7 0.2 reduce_sum.36
  237.0 0.5 copy-done.3
  237.5 0.1 maximum_convert_fusion
  237.6 0.0 copy-start.4
  237.6 0.5 fusion.34
  238.1 0.5 copy-done.4
  238.6 1.0 convert_bitcast_fusion
  239.6 0.2 copy.43
  239.8 1.3 collective-permute-start.1
  241.1 1.0 copy.37
  242.1 3.7 collective-permute-start
  245.8 6.3 %fusion.10 = f32[64,16,128]{2,1,0:T(8,128)} fusion(f32[128,64,16]{0,2,1:T(8,128)S(1)} %bitcast.81, f32[128,128,64]{1,0,2:T(8,128)} %copy.39, pred[128,128]{1,0:T(8,128)(4,1)S(1)} %get-tuple-element.26, pred[128,128]{1,0:T(8,128)(4,1)S(1)} %get-tuple-element.27), kind=kOutput, calls=%fused_computation.16 | convolution fusion | flops 203423744 | bytes 5275648 | tf_op jit(solution)/shard_map/nst,snc->tnc/dot_general | solution.py:95
  252.2 0.0 copy-done.1
  252.2 7.4 %fusion.11 = f32[64,16,128]{2,1,0:T(8,128)} fusion(f32[128,64,16]{0,2,1:T(8,128)S(1)} %bitcast.82, f32[128,128,64]{1,0,2:T(8,128)S(1)} %copy-done, pred[128,128]{1,0:T(8,128)(4,1)S(1)} %get-tuple-element.26, pred[128,128]{1,0:T(8,128)(4,1)S(1)} %get-tuple-element.27), kind=kOutput, calls=%fused_computation.17 | convolution fusion | flops 203423744 | bytes 5275648 | tf_op jit(solution)/shard_map/nst,tnc->snc/dot_general | solution.py:79
  259.6 0.0 collective-permute-done.1
  259.6 1.8 copy.44
  261.4 5.4 %fusion.46 = f32[64,16,128]{2,1,0:T(8,128)} fusion(f32[64,16,128]{2,1,0:T(8,128)S(1)} %copy-done.2, bf16[128,64,16]{0,2,1:T(8,128)(2,1)} %bitcast.89, f32[128,128,64]{1,0,2:T(8,128)} %copy.41, pred[128,128]{1,0:T(8,128)(4,1)S(1)} %get-tuple-element.29, pred[128,128]{1,0:T(8,128)(4,1)S(1)} %get-tuple-element.28), kind=kOutput, calls=%fused_computation.54 | convolution fusion | flops 203554816 | bytes 5537792 | tf_op jit(solution)/shard_map/nst,snc->tnc/dot_general | solution.py:99
  266.8 1.2 copy.45
  268.0 0.0 collective-permute-done
  268.0 1.8 copy.40
  269.8 6.6 %fusion.45 = f32[64,16,128]{2,1,0:T(8,128)} fusion(f32[64,16,128]{2,1,0:T(8,128)} %fusion.11, bf16[128,64,16]{0,2,1:T(8,128)(2,1)} %bitcast.88, f32[128,128,64]{1,0,2:T(8,128)} %copy.41, pred[128,128]{1,0:T(8,128)(4,1)S(1)} %get-tuple-element.29, pred[128,128]{1,0:T(8,128)(4,1)S(1)} %get-tuple-element.28), kind=kOutput, calls=%fused_computation.53 | convolution fusion | flops 203554816 | bytes 5537792 | tf_op jit(solution)/shard_map/nst,tnc->snc/dot_general | solution.py:83
  276.4 2.0 copy.42
  278.5 2.2 slice_multiply_fusion.5
  280.6 0.2 pad_maximum_fusion.1
  280.8 1.3 collective-permute-start.2
  282.1 2.3 collective-permute-done.2
  284.4 0.2 pad_maximum_fusion
  284.6 0.5 fusion.32
  285.1 0.4 copy.46
  285.5 1.2 copy.47
  286.7 0.0 all-gather.5.cloned.1.call-update
  286.7 0.0 reduce-scatter.2.cloned.1.call-start
  286.8 17.3 %copy.48 = bf16[2048,3,1024]{0,2,1:T(8,128)(2,1)} copy(bf16[2048,3,1024]{2,0,1:T(8,128)(2,1)} %param.10) | data formatting | bytes 25165824 | tf_op args[1]
  304.0 11.2 %all-gather.5.cloned.1.call-done = bf16[128,4,3072]{2,0,1:T(8,128)(2,1)} async-done(((bf16[128,1,3072]{2,0,1:T(8,128)(2,1)}), bf16[128,4,3072]{2,0,1:T(8,128)(2,1)}) %all-gather.5.cloned.1.call-update) | async-done | bytes 3145744 | tf_op jit(solution)/shard_map/all_gather | solution.py:115
  315.2 11.7 %convolution_convert_fusion = bf16[128,4,2048]{2,0,1:T(8,128)(2,1)} fusion(bf16[128,4,3072]{2,0,1:T(8,128)(2,1)} %all-gather.5.cloned.1.call-done, bf16[2048,3072,1]{0,1,2:T(8,128)(2,1)} %bitcast.78), kind=kOutput, calls=%fused_computation.20 | convolution fusion | flops 6443499520 | bytes 17825792 | tf_op jit(solution)/shard_map/dot_general | solution.py:123
  326.9 0.0 reduce-scatter.2.cloned.1.call-update
  326.9 11.5 %bitcast_convert_fusion = bf16[3072,2048]{1,0:T(8,128)(2,1)} fusion(bf16[128,4,3072]{2,0,1:T(8,128)(2,1)} %all-gather.5.cloned.1.call-done, bf16[128,4,2048]{2,0,1:T(8,128)(2,1)S(1)} %copy-done.7), kind=kOutput, calls=%fused_computation.2 | convolution fusion | flops 6448742400 | bytes 17825792 | tf_op jit(solution)/shard_map/dot_general | solution.py:117
  338.5 16.7 %copy.52 = bf16[2048,3,1024]{2,0,1:T(8,128)(2,1)} copy(bf16[2048,3,1024]{0,2,1:T(8,128)(2,1)} %bitcast.79) | data formatting | bytes 25165824
  355.1 40.2 %reduce-scatter.2.cloned.1.call-done = bf16[16,4,2048]{2,0,1:T(8,128)(2,1)} async-done(((bf16[128,4,2048]{2,0,1:T(8,128)(2,1)}), bf16[16,4,2048]{2,0,1:T(8,128)(2,1)}) %reduce-scatter.2.cloned.1.call-update) | async-done | bytes 262160 | tf_op jit(solution)/shard_map/reduce_scatter | solution.py:126
  395.4 1.9 copy.51
  (19 shorter events, 0.2 us)
Async XLA Ops:
  7.2 55.6 %all-gather.3.cloned.1.call-start = ((), (), s32[]{:S(2)}) async-start(), calls=%async_computation.4 | async-start | bytes 2359296 | tf_op jit(solution)/shard_map/all_gather | solution.py:32
  70.0 18.7 %all-to-all-start.2 = ((bf16[130,4,1024]{2,0,1:T(8,128)(2,1)}), bf16[130,4,1024]{2,0,1:T(8,128)(2,1)S(1)}, u32[]{:S(2)}, u32[]{:S(2)}) async-start(bf16[130,4,1024]{2,0,1:T(8,128)(2,1)} %fusion.42), calls=%async_computation.2 | async-start | bytes 2228224 | tf_op jit(solution)/shard_map/all_to_all | solution.py:55
  88.6 18.7 %all-to-all-start.1 = ((bf16[130,4,1024]{2,0,1:T(8,128)(2,1)}), bf16[130,4,1024]{2,0,1:T(8,128)(2,1)S(1)}, u32[]{:S(2)}, u32[]{:S(2)}) async-start(bf16[130,4,1024]{2,0,1:T(8,128)(2,1)} %fusion.39), calls=%async_computation.1 | async-start | bytes 2228224 | tf_op jit(solution)/shard_map/all_to_all | solution.py:52
  107.3 129.4 %all-to-all-start = ((bf16[130,4,1024]{2,0,1:T(8,128)(2,1)}), bf16[130,4,1024]{2,0,1:T(8,128)(2,1)S(1)}, u32[]{:S(2)}, u32[]{:S(2)}) async-start(bf16[130,4,1024]{2,0,1:T(8,128)(2,1)} %fusion.36), calls=%async_computation | async-start | bytes 2228224 | tf_op jit(solution)/shard_map/all_to_all | solution.py:49
  110.8 204.4 %all-gather.5.cloned.1.call-start = ((), (), s32[]{:S(2)}) async-start(), calls=%async_computation.5 | async-start | bytes 3932160 | tf_op jit(solution)/shard_map/all_gather | solution.py:115
  228.1 7.4 %copy-start.5 = (f32[3,3,1024]{2,1,0:T(4,128)S(1)}, f32[3,3,1024]{2,1,0:T(4,128)}, u32[]{:S(2)}) copy-start(f32[3,3,1024]{2,1,0:T(4,128)} %param.11) | copy-start | bytes 110596
  236.5 1.0 copy-start.3
  237.6 1.0 copy-start.4
  239.8 19.8 %collective-permute-start.1 = (bf16[128,1024]{1,0:T(8,128)(2,1)}, bf16[128,1024]{1,0:T(8,128)(2,1)}, u32[]{:S(2)}, u32[]{:S(2)}) collective-permute-start(bf16[128,1024]{1,0:T(8,128)(2,1)} %get-tuple-element.13), channel_id=1, source_target_pairs={{8,0},{16,8},{24,16},{9,1},{17,9},{25,17},{10,2},{18,10},{26,18},{... | collective-permute-start | bytes 786440 | tf_op jit(solution)/shard_map/ppermute | solution.py:10
  242.1 25.9 %collective-permute-start = (bf16[128,1024]{1,0:T(8,128)(2,1)}, bf16[128,1024]{1,0:T(8,128)(2,1)}, u32[]{:S(2)}, u32[]{:S(2)}) collective-permute-start(bf16[128,1024]{1,0:T(8,128)(2,1)} %get-tuple-element.20), channel_id=1, source_target_pairs={{0,8},{8,16},{16,24},{1,9},{9,17},{17,25},{2,10},{10,18},{18,26},{... | collective-permute-start | bytes 786440 | tf_op jit(solution)/shard_map/ppermute | solution.py:10
  245.8 6.4 %copy-start = (f32[128,128,64]{1,0,2:T(8,128)S(1)}, f32[128,128,64]{1,0,2:T(8,128)}, u32[]{:S(2)}) copy-start(f32[128,128,64]{1,0,2:T(8,128)} %copy.39) | copy-start | bytes 12582916
  245.8 6.4 %copy-start.1 = (f32[128,1,1024]{0,2,1:T(8,128)S(1)}, f32[128,1,1024]{0,2,1:T(8,128)}, u32[]{:S(2)}) copy-start(f32[128,1,1024]{0,2,1:T(8,128)} %copy.37) | copy-start | bytes 1572868
  252.2 9.2 %copy-start.2 = (f32[64,16,128]{2,1,0:T(8,128)S(1)}, f32[64,16,128]{2,1,0:T(8,128)}, u32[]{:S(2)}) copy-start(f32[64,16,128]{2,1,0:T(8,128)} %fusion.10) | copy-start | bytes 1572868
  269.8 8.6 %copy-start.6 = (f32[1024]{0:T(1024)S(1)}, f32[1024]{0:T(1024)}, u32[]{:S(2)}) copy-start(f32[1024]{0:T(1024)} %param.14) | copy-start | bytes 12292
  280.8 3.6 collective-permute-start.2
  286.7 108.6 %reduce-scatter.2.cloned.1.call-start = ((), (), s32[]{:S(2)}) async-start(), calls=%async_computation.6 | async-start | bytes 2359296 | tf_op jit(solution)/shard_map/reduce_scatter | solution.py:126
  315.2 11.7 %copy-start.7 = (bf16[128,4,2048]{2,0,1:T(8,128)(2,1)S(1)}, bf16[128,4,2048]{2,0,1:T(8,128)(2,1)}, u32[]{:S(2)}) copy-start(bf16[128,4,2048]{2,0,1:T(8,128)(2,1)} %all-gather.3.cloned.1.call-done) | copy-start | bytes 6291460
Sparse Core Ops, SparseCore 0:
  10.8 51.9 all-gather.2
  286.8 28.3 all-gather.4
  327.0 68.2 reduce-scatter.1
where the time goes:
time: 405 us; the launch traced here: 404 us
  local copies, waits for them, and re-layouts  174 us (43%)
  waiting for transfers between devices  123 us (30%)
  matrix products  67.9 us (17%)
  starting transfers between devices  17 us (4%)
  between operations  14 us (3%)
  other arithmetic  7 us (2%)
    gather x2, local copies, waits for them, and re-layouts, toeplitz_pair(): near_taken = jnp.take(kernel, jnp.clip(lag_grid, 0, tap_count - 1), axis=1)  62.3 us
    gather x2, local copies, waits for them, and re-layouts, toeplitz_pair(): far_taken = jnp.take(kernel, jnp.clip(far_grid, 0, tap_count - 1), axis=1)  62.2 us
    all_gather x1, waiting for transfers between devices, shards(): gathered = lax.all_gather(inputs, 'tp', axis=0, tiled=True)  52.2 us
    reduce_scatter x1, waiting for transfers between devices, shards(): lax.psum_scatter(result.reshape(own_count * lax.axis_size('tp'), blocks,...  40.2 us
    unnamed x21, local copies, waits for them, and re-layouts  39.4 us
    dot_general x3, matrix products, shards(): jnp.dot(flat_ext, featurizer[:, stream, :], preferred_element_type=jnp.fl...  18.9 us
    dot_general x1, matrix products, shards(): lax.dot_general(flat_piece, weight_block, (((1,), (1,)), ((), ())), prefe...  11.7 us
    dot_general x1, matrix products, shards(): lax.dot_general(gathered, grad_all, (((0, 1), (0, 1)), ((), ())), preferr...  11.5 us
  transfers between devices with their start and end apart: 9, of which 6 were waited for; matrix products, arithmetic and copies ran while one was open for 52% of the time, Pallas kernels for 0%

commit v1 on v0

v1 whole, which is shorter than its diff:
```python
import functools

import jax
import jax.numpy as jnp
from jax import lax
from jax.experimental import pallas as pl
from jax.experimental.pallas import tpu as pltpu
from jax.sharding import PartitionSpec as P

F32 = jnp.float32
BF16 = jnp.bfloat16
MESH = pl.DeviceIdType.MESH
VMEM = pl.BlockSpec(memory_space=pltpu.VMEM)
LANES = 128
HALO = 16
HEAD = 8


def hyena_kernel(
    blocks, width, feat, short, taps, taps_back, skip, upstream, out, grad,
    ext_p, ext_g, query, key, value, prod, conv_grad, filt_grad, sems, head_sems,
):
    me = lax.axis_index("fsdp")
    rest = lax.axis_index("tp")
    tokens, channels = out.shape
    taps_count = taps.shape[1]
    has_prev = me > 0
    has_next = me < blocks - 1
    prev = jnp.maximum(me - 1, 0)
    later = jnp.minimum(me + 1, blocks - 1)
    barrier = pltpu.get_barrier_semaphore()

    for peer in (lax.rem(me + 1, blocks), lax.rem(me + blocks - 1, blocks)):
        pl.semaphore_signal(barrier, inc=1, device_id=(peer, rest), device_id_type=MESH)
    pl.semaphore_wait(barrier, 2)

    def front(at, _):
        cols = pl.ds(pl.multiple_of(at * LANES, LANES), LANES)
        parts = []
        for i in range(3):
            f = feat[i, :, cols].astype(F32)
            acc = short[pl.ds(i, 1), cols] * f[HALO:]
            for j in range(1, 3):
                acc = acc + short[pl.ds(3 * j + i, 1), cols] * pltpu.roll(f, j, 0)[HALO:]
            parts.append(acc)
        p = parts[1] * parts[2]
        cg = upstream[:, cols].astype(F32) * parts[0]
        query[:, cols] = parts[0]
        key[:, cols] = parts[1]
        value[:, cols] = parts[2]
        prod[:, cols] = p
        conv_grad[:, cols] = cg
        ext_p[pl.ds(tokens, tokens), cols] = p.astype(BF16)
        ext_g[pl.ds(0, tokens), cols] = cg.astype(BF16)
        return 0

    lax.fori_loop(0, channels // LANES, front, 0)

    to_next = pltpu.make_async_remote_copy(
        src_ref=ext_p.at[pl.ds(tokens, tokens)], dst_ref=ext_p.at[pl.ds(0, tokens)],
        send_sem=sems.at[0], recv_sem=sems.at[1], device_id=(later, rest), device_id_type=MESH)
    to_prev = pltpu.make_async_remote_copy(
        src_ref=ext_g.at[pl.ds(0, tokens)], dst_ref=ext_g.at[pl.ds(tokens, tokens)],
        send_sem=sems.at[2], recv_sem=sems.at[3], device_id=(prev, rest), device_id_type=MESH)

    @pl.when(has_next)
    def _():
        to_next.start()

    @pl.when(has_prev)
    def _():
        to_prev.start()

    @pl.when(jnp.logical_not(has_prev))
    def _():
        ext_p[pl.ds(0, tokens), :] = jnp.zeros((tokens, channels), BF16)

    @pl.when(jnp.logical_not(has_next))
    def _():
        ext_g[pl.ds(tokens, tokens), :] = jnp.zeros((tokens, channels), BF16)

    @pl.when(has_prev)
    def _():
        to_next.wait_recv()

    @pl.when(has_next)
    def _():
        to_prev.wait_recv()

    per_tile = LANES // width
    lane = lax.broadcasted_iota(jnp.int32, (tokens, LANES), 1) // width

    def mixed(rows, ext, first):
        acc = None
        for g in range(per_tile):
            line = jnp.concatenate([rows[g : g + 1], jnp.zeros((1, 2 * tokens - taps_count), F32)], axis=1)
            wide = jnp.broadcast_to(line, (tokens, 2 * tokens))
            toeplitz = pltpu.roll(wide, first, 1, stride=1, stride_axis=0).astype(BF16)
            part = jnp.dot(toeplitz, ext, preferred_element_type=F32)
            acc = part if acc is None else jnp.where(lane == g, part, acc)
        return acc

    def back(at, _):
        cols = pl.ds(pl.multiple_of(at * LANES, LANES), LANES)
        rows = pl.ds(pl.multiple_of(at * per_tile, per_tile), per_tile)
        gain = skip[:, cols]
        conv = mixed(taps_back[rows, :], ext_p[:, cols], 1 + tokens - taps_count) + gain * prod[:, cols]
        pg = mixed(taps[rows, :], ext_g[:, cols], 0) + gain * conv_grad[:, cols]
        out[:, cols] = (query[:, cols] * conv).astype(BF16)
        own = pl.ds(0, tokens)
        filt_grad[0, own, cols] = upstream[:, cols].astype(F32) * conv
        filt_grad[1, own, cols] = pg * value[:, cols]
        filt_grad[2, own, cols] = pg * key[:, cols]
        return 0

    lax.fori_loop(0, channels // LANES, back, 0)

    head = pltpu.make_async_remote_copy(
        src_ref=filt_grad.at[:, pl.ds(0, HEAD)], dst_ref=filt_grad.at[:, pl.ds(tokens, HEAD)],
        send_sem=head_sems.at[0], recv_sem=head_sems.at[1], device_id=(prev, rest), device_id_type=MESH)

    @pl.when(has_prev)
    def _():
        head.start()

    @pl.when(jnp.logical_not(has_next))
    def _():
        filt_grad[:, pl.ds(tokens, HEAD), :] = jnp.zeros((3, HEAD, channels), F32)

    @pl.when(has_next)
    def _():
        head.wait_recv()

    def last(at, _):
        cols = pl.ds(pl.multiple_of(at * LANES, LANES), LANES)
        for i in range(3):
            f = filt_grad[i, :, cols]
            acc = short[pl.ds(i, 1), cols] * f[:tokens]
            for j in range(1, 3):
                acc = acc + short[pl.ds(3 * j + i, 1), cols] * pltpu.roll(f, tokens + HEAD - j, 0)[:tokens]
            grad[i, :, cols] = acc.astype(BF16)
        return 0

    lax.fori_loop(0, channels // LANES, last, 0)

    @pl.when(has_next)
    def _():
        to_next.wait_send()

    @pl.when(has_prev)
    def _():
        to_prev.wait_send()
        head.wait_send()


def hyena(feat, short_filter, long_filter, decay_rate, skip_gain, upstream):
    tokens, channels = upstream.shape
    taps = long_filter * jnp.exp(-decay_rate[:, None] * jnp.arange(long_filter.shape[1]).astype(F32)[None, :])
    width = channels // long_filter.shape[0]
    wide = pltpu.VMEM((tokens, channels), F32)
    return pl.pallas_call(
        functools.partial(hyena_kernel, lax.axis_size("fsdp"), width),
        out_shape=(jax.ShapeDtypeStruct((tokens, channels), BF16), jax.ShapeDtypeStruct((3, tokens, channels), BF16)),
        in_specs=[VMEM] * 6,
        out_specs=(VMEM, VMEM),
        scratch_shapes=[
            pltpu.VMEM((2 * tokens, channels), BF16), pltpu.VMEM((2 * tokens, channels), BF16),
            wide, wide, wide, wide, wide, pltpu.VMEM((3, tokens + HEAD, channels), F32),
            pltpu.SemaphoreType.DMA((4,)), pltpu.SemaphoreType.DMA((2,)),
        ],
        compiler_params=pltpu.CompilerParams(collective_id=1, has_side_effects=True, vmem_limit_bytes=40 * 2**20),
    )(feat, short_filter.reshape(9, channels), taps, taps[:, ::-1], skip_gain[None], upstream)


def weight_kernel(x, g, out):
    out[...] = lax.dot_general(x[...], g[...], (((0,), (0,)), ((), ())), preferred_element_type=F32).astype(BF16)


def weight_product(x, grads):
    rows, depth = x.shape
    channels = grads.shape[2]
    step = min(512, depth)
    return pl.pallas_call(
        weight_kernel,
        grid=(depth // step, 3),
        out_shape=jax.ShapeDtypeStruct((3, depth, channels), BF16),
        in_specs=[
            pl.BlockSpec((rows, step), lambda d, i: (0, d)),
            pl.BlockSpec((None, rows, channels), lambda d, i: (i, 0, 0)),
        ],
        out_specs=pl.BlockSpec((None, step, channels), lambda d, i: (i, d, 0)),
        compiler_params=pltpu.CompilerParams(vmem_limit_bytes=40 * 2**20),
        cost_estimate=pl.CostEstimate(
            flops=6 * rows * depth * channels, bytes_accessed=2 * 3 * depth * channels, transcendentals=0),
    )(x, grads)


def shards(inputs, featurizer, short_filter, long_filter, decay_rate, skip_gain, output_grad):
    weights = featurizer.transpose(1, 0, 2)
    gathered = lax.all_gather(inputs.transpose(1, 0, 2), "tp", axis=1, tiled=True)
    blocks, tokens, depth = gathered.shape
    channels = weights.shape[2]
    border = jnp.zeros((1, HALO, depth), BF16)
    earlier = jnp.concatenate([border, gathered[: blocks - 1, tokens - HALO :]], axis=0)
    extended = jnp.concatenate([earlier, gathered], axis=1).reshape(blocks * (tokens + HALO), depth)
    feats = []
    for i in range(3):
        part = jnp.dot(extended, weights[i], preferred_element_type=F32).astype(BF16)
        part = part.reshape(blocks, tokens + HALO, channels)
        swapped = lax.all_to_all(part, "fsdp", split_axis=0, concat_axis=0, tiled=True)
        feats.append(jnp.sum(swapped.astype(F32), axis=0).astype(BF16))
    out, own_grad = hyena(
        jnp.stack(feats), short_filter, long_filter, decay_rate, skip_gain, output_grad.reshape(tokens, channels))
    grads = lax.all_gather(own_grad, "fsdp", axis=1, tiled=True)
    turned = grads.reshape(3, blocks, tokens, channels).transpose(0, 2, 1, 3).reshape(grads.shape)
    part = None
    for i in range(3):
        term = lax.dot_general(turned[i], weights[i], (((1,), (1,)), ((), ())), preferred_element_type=F32)
        part = term if part is None else part + term
    weight_grad = weight_product(gathered.reshape(blocks * tokens, depth), grads)
    input_grad = lax.psum_scatter(
        part.astype(BF16).reshape(tokens, blocks, depth), "tp", scatter_dimension=0, tiled=True)
    return out.reshape(output_grad.shape), input_grad, weight_grad.transpose(1, 0, 2)


def solution(mesh):
    in_specs = (
        P("tp", None, "fsdp"),
        P("fsdp", None, "tp"),
        P(None, None, "tp"),
        P("tp", None),
        P("tp"),
        P("tp"),
        P(None, "fsdp", "tp"),
    )
    out_specs = (P(None, "fsdp", "tp"), P("tp", None, "fsdp"), P("fsdp", None, "tp"))
    return jax.shard_map(shards, mesh=mesh, in_specs=in_specs, out_specs=out_specs, check_vma=False)
```

time: 405 us -> 312 us (0.77)
  local copies, waits for them, and re-layouts: 174 us -> 18.9 us
  waiting for transfers between devices: 123 us -> 204 us
  matrix products: 67.9 us -> 34.1 us
  Pallas kernels: 0 us -> 23.9 us
  starting transfers between devices: 17 us -> 11.7 us
    gather x4 -> x0, local copies, waits for them, and re-layouts: 124 us -> none  [the longest x2 62.3 us: toeplitz_pair(): near_taken = jnp.take(kernel, jnp.clip(lag_grid, 0, tap_count - 1), axis=1)]
    unnamed x3 -> x4, waiting for transfers between devices: 0.05 us -> 88.1 us
    reduce_scatter x1 -> x0, waiting for transfers between devices: 40.2 us -> none  [shards(): lax.psum_scatter(result.reshape(own_count * lax.axis_size('tp'), blocks,...]
    dot_general x9 -> x6, matrix products: 67.9 us -> 34.1 us  [the longest x3 19 us: shards(): jnp.dot(extended, weights[i], preferred_element_type=F32).astype(BF16)]
    unnamed x21 -> x24, local copies, waits for them, and re-layouts: 39.4 us -> 6.47 us
    pallas_call x0 -> x2, Pallas kernels: none -> 23.9 us  [the longest x1 12.7 us: hyena(): pl.pallas_call(functools.partial(hyena_kernel, lax.axis_size('fsdp'), wid...]
    all_gather x2, waiting for transfers between devices: 63.4 us -> 81.8 us  [the longest x1 53.7 us: shards(): lax.all_gather(inputs.transpose(1, 0, 2), 'tp', axis=1, tiled=True)]
    all_to_all x3, waiting for transfers between devices: 17.5 us -> 34.4 us  [shards(): lax.all_to_all(part, 'fsdp', split_axis=0, concat_axis=0, tiled=True)]
  transfers between devices with their start and end apart: 9 -> 6, of which waited for: 6 -> 6; matrix products, arithmetic and copies ran while one was open for 52% -> 4% of each run, Pallas kernels for 0% -> 4%
where the time goes in v1:
time: 312 us
  waiting for transfers between devices  204 us (65%)
  matrix products  34.1 us (11%)
  Pallas kernels  23.9 us (8%)
  local copies, waits for them, and re-layouts  18.9 us (6%)
  between operations  14.7 us (5%)
  starting transfers between devices  11.7 us (4%)
  other arithmetic  3.91 us (1%)
    unnamed x4, waiting for transfers between devices  88.1 us
    all_gather x1, waiting for transfers between devices, shards(): lax.all_gather(inputs.transpose(1, 0, 2), 'tp', axis=1, tiled=True)  53.7 us
    all_to_all x3, waiting for transfers between devices, shards(): lax.all_to_all(part, 'fsdp', split_axis=0, concat_axis=0, tiled=True)  34.4 us
    all_gather x1, waiting for transfers between devices, shards(): grads = lax.all_gather(own_grad, 'fsdp', axis=1, tiled=True)  28.1 us
    dot_general x3, matrix products, shards(): jnp.dot(extended, weights[i], preferred_element_type=F32).astype(BF16)  19 us
    dot_general x3, matrix products, shards(): lax.dot_general(turned[i], weights[i], (((1,), (1,)), ((), ())), preferre...  15.1 us
    pallas_call x1, Pallas kernels, hyena(): pl.pallas_call(functools.partial(hyena_kernel, lax.axis_size('fsdp'), wid...  12.7 us
    all_to_all x3, starting transfers between devices, shards(): lax.all_to_all(part, 'fsdp', split_axis=0, concat_axis=0, tiled=True)  11.4 us
  transfers between devices with their start and end apart: 6, of which 6 were waited for; matrix products, arithmetic and copies ran while one was open for 4% of the time, Pallas kernels for 4%

profile of v1, /device:TPU:0, one launch (start us, length us, event | category | flops | bytes accessed | tf_op | source)
XLA Modules:
  0.0 311.6 jit_solution(17819115567208802509)
XLA Ops:
  7.2 0.0 all-gather.3.cloned.1.call-start
  7.2 1.8 copy.18
  9.0 0.0 all-gather.3.cloned.1.call-update
  9.0 53.7 %all-gather.3.cloned.1.call-done = bf16[4,128,2048]{2,1,0:T(8,128)(2,1)} async-done(((bf16[4,16,2048]{2,1,0:T(8,128)(2,1)}), bf16[4,128,2048]{2,1,0:T(8,128)(2,1)}) %all-gather.3.cloned.1.call-update) | async-done | bytes 2097168 | tf_op jit(solution)/shard_map/all_gather | solution.py:200
  62.8 0.9 slice.34
  63.7 1.8 fusion.7
  65.5 0.0 copy-start.4
  65.5 6.7 %fusion.8 = bf16[576,1024]{1,0:T(8,128)(2,1)} fusion(bf16[576,2048]{1,0:T(8,128)(2,1)S(1)} %bitcast.53, bf16[3,2048,1024]{2,1,0:T(8,128)(2,1)} %bitcast.63), kind=kOutput, calls=%fused_computation.14 | convolution fusion | flops 2416508928 | bytes 7733248 | tf_op jit(solution)/shard_map/dot_general | solution.py:208
  72.1 3.5 %all-to-all-start.2 = ((bf16[4,144,1024]{2,1,0:T(8,128)(2,1)}), bf16[4,144,1024]{2,1,0:T(8,128)(2,1)S(1)}, u32[]{:S(2)}, u32[]{:S(2)}) async-start(bf16[4,144,1024]{2,1,0:T(8,128)(2,1)} %bitcast.58), calls=%async_computation.2 | async-start | bytes 2359296 | tf_op jit(solution)/shard_map/all_to_all | solution.py:210
  75.7 0.0 copy-done.4
  75.7 5.8 %fusion.9 = bf16[576,1024]{1,0:T(8,128)(2,1)} fusion(bf16[576,2048]{1,0:T(8,128)(2,1)S(1)} %bitcast.54, bf16[3,2048,1024]{2,1,0:T(8,128)(2,1)} %bitcast.64), kind=kOutput, calls=%fused_computation.15 | convolution fusion | flops 2416508928 | bytes 7733248 | tf_op jit(solution)/shard_map/dot_general | solution.py:208
  81.5 10.0 %all-to-all-done.2 = bf16[4,144,1024]{2,1,0:T(8,128)(2,1)S(1)} async-done(((bf16[4,144,1024]{2,1,0:T(8,128)(2,1)}), bf16[4,144,1024]{2,1,0:T(8,128)(2,1)S(1)}, u32[]{:S(2)}, u32[]{:S(2)}) %all-to-all-start.2) | async-done | bytes 1179680 | tf_op jit(solution)/shard_map/all_to_all | solution.py:210
  91.5 3.5 %all-to-all-start.1 = ((bf16[4,144,1024]{2,1,0:T(8,128)(2,1)}), bf16[4,144,1024]{2,1,0:T(8,128)(2,1)S(1)}, u32[]{:S(2)}, u32[]{:S(2)}) async-start(bf16[4,144,1024]{2,1,0:T(8,128)(2,1)} %bitcast.57), calls=%async_computation.1 | async-start | bytes 2359296 | tf_op jit(solution)/shard_map/all_to_all | solution.py:210
  95.1 0.0 copy-start.8
  95.1 0.0 copy-start.7
  95.1 0.0 copy-start.6
  95.1 6.5 %fusion.10 = bf16[576,1024]{1,0:T(8,128)(2,1)} fusion(bf16[576,2048]{1,0:T(8,128)(2,1)} %bitcast.55, bf16[3,2048,1024]{2,1,0:T(8,128)(2,1)} %bitcast.65), kind=kOutput, calls=%fused_computation.16 | convolution fusion | flops 2416508928 | bytes 7733248 | tf_op jit(solution)/shard_map/dot_general | solution.py:208
  101.6 9.3 %all-to-all-done.1 = bf16[4,144,1024]{2,1,0:T(8,128)(2,1)S(1)} async-done(((bf16[4,144,1024]{2,1,0:T(8,128)(2,1)}), bf16[4,144,1024]{2,1,0:T(8,128)(2,1)S(1)}, u32[]{:S(2)}, u32[]{:S(2)}) %all-to-all-start.1) | async-done | bytes 1179680 | tf_op jit(solution)/shard_map/all_to_all | solution.py:210
  110.9 0.0 copy-start.2
  110.9 0.0 copy-start.3
  110.9 4.4 %all-to-all-start = ((bf16[4,144,1024]{2,1,0:T(8,128)(2,1)}), bf16[4,144,1024]{2,1,0:T(8,128)(2,1)}, u32[]{:S(2)}, u32[]{:S(2)}) async-start(bf16[4,144,1024]{2,1,0:T(8,128)(2,1)} %bitcast.56), calls=%async_computation | async-start | bytes 2359296 | tf_op jit(solution)/shard_map/all_to_all | solution.py:210
  115.3 0.0 all-gather.5.cloned.1.call-start
  115.3 0.0 copy-done.8
  115.4 0.0 copy-done.7
  115.4 0.1 exponential_multiply_fusion.taps
  115.5 0.1 rev.3.taps_back
  115.5 0.0 copy-done.6
  115.6 0.2 reduce_sum.38
  115.8 0.2 reduce_sum.37
  116.0 15.2 %all-to-all-done = bf16[4,144,1024]{2,1,0:T(8,128)(2,1)} async-done(((bf16[4,144,1024]{2,1,0:T(8,128)(2,1)}), bf16[4,144,1024]{2,1,0:T(8,128)(2,1)}, u32[]{:S(2)}, u32[]{:S(2)}) %all-to-all-start) | async-done | bytes 1179680 | tf_op jit(solution)/shard_map/all_to_all | solution.py:210
  131.2 1.5 reduce_sum.36
  132.7 0.1 pad_maximum_fusion.feat
  132.8 0.0 copy-done.2
  132.8 0.0 copy-done.3
  132.8 12.7 %shard_map.94 = (bf16[128,1024]{1,0:T(8,128)(2,1)S(1)}, bf16[3,128,1024]{2,1,0:T(8,128)(2,1)}) custom-call(bf16[3,144,1024]{2,1,0:T(8,128)(2,1)S(1)} %pad_maximum_fusion.feat, f32[9,1024]{1,0:T(8,128)S(1)} %reshape.53.short, f32[64,128]{1,0:T(8,128)S(1)} %exponential_multiply_fusion.taps, f32[64,128]{1,0:T(8,128)S(1)} %rev.3.taps_back, ...), custom_call_target="tpu_custom_call" | custom-call | tf_op jit(solution)/shard_map/pallas_call | solution.py:161
  145.6 0.0 all-gather.5.cloned.1.call-update
  145.6 0.2 all-reduce.4.cloned.1.call-start
  145.9 28.1 %all-gather.5.cloned.1.call-done.g = bf16[3,512,1024]{2,1,0:T(8,128)(2,1)} async-done(((bf16[3,128,1024]{2,1,0:T(8,128)(2,1)}), bf16[3,512,1024]{2,1,0:T(8,128)(2,1)}) %all-gather.5.cloned.1.call-update) | async-done | bytes 3145744 | tf_op jit(solution)/shard_map/all_gather | solution.py:214
  173.9 4.3 %copy.17 = bf16[3,4,128,1024]{3,1,2,0:T(4,128)(2,1)S(1)} copy(bf16[3,4,128,1024]{3,2,1,0:T(8,128)(2,1)} %bitcast.47) | data formatting | bytes 6291456 | tf_op jit(solution)/shard_map/reshape | solution.py:215
  178.2 1.2 fusion.11
  179.4 1.1 squeeze.26
  180.6 0.3 squeeze.25
  180.8 0.3 squeeze.24
  181.1 4.6 %fusion.1 = f32[512,2048]{1,0:T(8,128)S(1)} fusion(bf16[512,1024]{1,0:T(8,128)(2,1)S(1)} %squeeze.24, bf16[3,2048,1024]{2,1,0:T(8,128)(2,1)} %bitcast.66), kind=kOutput, calls=%fused_computation.6 | convolution fusion | flops 2147483648 | bytes 9437184 | tf_op jit(solution)/shard_map/dot_general | solution.py:218
  185.7 0.0 copy-start.5
  185.7 4.6 %fusion.3 = f32[512,2048]{1,0:T(8,128)S(1)} fusion(bf16[512,1024]{1,0:T(8,128)(2,1)S(1)} %squeeze.25, bf16[3,2048,1024]{2,1,0:T(8,128)(2,1)} %bitcast.67), kind=kOutput, calls=%fused_computation.8 | convolution fusion | flops 2147483648 | bytes 9437184 | tf_op jit(solution)/shard_map/dot_general | solution.py:218
  190.3 0.0 copy-done.5
  190.3 5.9 %add_convert_fusion = bf16[512,2048]{1,0:T(8,128)(2,1)} fusion(f32[512,2048]{1,0:T(8,128)S(1)} %fusion.1, f32[512,2048]{1,0:T(8,128)S(1)} %fusion.3, bf16[512,1024]{1,0:T(8,128)(2,1)S(1)} %copy-done.5, bf16[3,2048,1024]{2,1,0:T(8,128)(2,1)} %bitcast.68), kind=kOutput, calls=%fused_computation.5 | convolution fusion | flops 2150629376 | bytes 15728640 | tf_op jit(solution)/shard_map/dot_general | solution.py:218
  196.2 0.0 copy-start.9
  196.2 0.0 copy-start
  196.2 4.3 %reshape.57 = bf16[128,4,2048]{2,1,0:T(4,128)(2,1)} reshape(bf16[512,2048]{1,0:T(8,128)(2,1)} %add_convert_fusion) | data formatting | bytes 4194304 | tf_op jit(solution)/shard_map/reshape | solution.py:222
  200.5 0.0 all-reduce.4.cloned.1.call-update
  200.5 0.0 copy-done.9
  200.6 0.6 dynamic-slice
  201.8 0.0 copy-done
  201.8 0.0 copy-start.1
  201.8 1.6 copy-done.1
  203.4 11.1 %shard_map.95 = bf16[3,2048,1024]{2,1,0:T(8,128)(2,1)} custom-call(bf16[512,2048]{1,0:T(8,128)(2,1)S(1)} %bitcast.48, bf16[3,512,1024]{2,1,0:T(8,128)(2,1)S(1)} %copy-done), custom_call_target="tpu_custom_call" | custom-call | flops 6442450944 | bytes 12582912 | tf_op jit(solution)/shard_map/pallas_call | solution.py:183
  214.5 88.0 %all-reduce.4.cloned.1.call-done = bf16[128,4,2048]{2,1,0:T(4,128)(2,1)} async-done(((bf16[128,4,2048]{2,1,0:T(4,128)(2,1)}), bf16[128,4,2048]{2,1,0:T(4,128)(2,1)}) %all-reduce.4.cloned.1.call-update) | async-done | bytes 2097168
  302.6 1.8 constant_dynamic-slice_fusion
  304.3 0.7 copy.21
  (3 shorter events, 0.0 us)
Async XLA Ops:
  7.2 55.6 %all-gather.3.cloned.1.call-start = ((), (), s32[]{:S(2)}) async-start(), calls=%async_computation.3 | async-start | bytes 2359296 | tf_op jit(solution)/shard_map/all_gather | solution.py:200
  65.5 10.2 %copy-start.4 = (bf16[4,144,2048]{2,1,0:T(8,128)(2,1)}, bf16[4,144,2048]{2,1,0:T(8,128)(2,1)S(1)}, u32[]{:S(2)}) copy-start(bf16[4,144,2048]{2,1,0:T(8,128)(2,1)S(1)} %fusion.7) | copy-start | bytes 7077892
  72.1 19.4 %all-to-all-start.2 = ((bf16[4,144,1024]{2,1,0:T(8,128)(2,1)}), bf16[4,144,1024]{2,1,0:T(8,128)(2,1)S(1)}, u32[]{:S(2)}, u32[]{:S(2)}) async-start(bf16[4,144,1024]{2,1,0:T(8,128)(2,1)} %bitcast.58), calls=%async_computation.2 | async-start | bytes 2359296 | tf_op jit(solution)/shard_map/all_to_all | solution.py:210
  91.5 19.4 %all-to-all-start.1 = ((bf16[4,144,1024]{2,1,0:T(8,128)(2,1)}), bf16[4,144,1024]{2,1,0:T(8,128)(2,1)S(1)}, u32[]{:S(2)}, u32[]{:S(2)}) async-start(bf16[4,144,1024]{2,1,0:T(8,128)(2,1)} %bitcast.57), calls=%async_computation.1 | async-start | bytes 2359296 | tf_op jit(solution)/shard_map/all_to_all | solution.py:210
  95.1 20.3 %copy-start.8 = (f32[64]{0:T(128)S(1)}, f32[64]{0:T(128)}, u32[]{:S(2)}) copy-start(f32[64]{0:T(128)} %param.11) | copy-start | bytes 772
  95.1 20.3 %copy-start.7 = (f32[64,128]{1,0:T(8,128)S(1)}, f32[64,128]{1,0:T(8,128)}, u32[]{:S(2)}) copy-start(f32[64,128]{1,0:T(8,128)} %param.10) | copy-start | bytes 98308
  95.1 20.5 %copy-start.6 = (f32[3,3,1024]{2,1,0:T(4,128)S(1)}, f32[3,3,1024]{2,1,0:T(4,128)}, u32[]{:S(2)}) copy-start(f32[3,3,1024]{2,1,0:T(4,128)} %param.9) | copy-start | bytes 110596
  110.9 21.9 %copy-start.2 = (bf16[128,1,1024]{2,0,1:T(8,128)(2,1)S(1)}, bf16[128,1,1024]{2,0,1:T(8,128)(2,1)}, u32[]{:S(2)}) copy-start(bf16[128,1,1024]{2,0,1:T(8,128)(2,1)} %param.13) | copy-start | bytes 786436
  110.9 21.9 %copy-start.3 = (f32[1024]{0:T(1024)S(1)}, f32[1024]{0:T(1024)}, u32[]{:S(2)}) copy-start(f32[1024]{0:T(1024)} %param.12) | copy-start | bytes 12292
  110.9 20.3 %all-to-all-start = ((bf16[4,144,1024]{2,1,0:T(8,128)(2,1)}), bf16[4,144,1024]{2,1,0:T(8,128)(2,1)}, u32[]{:S(2)}, u32[]{:S(2)}) async-start(bf16[4,144,1024]{2,1,0:T(8,128)(2,1)} %bitcast.56), calls=%async_computation | async-start | bytes 2359296 | tf_op jit(solution)/shard_map/all_to_all | solution.py:210
  115.3 58.6 %all-gather.5.cloned.1.call-start = ((), (), s32[]{:S(2)}) async-start(), calls=%async_computation.4 | async-start | bytes 3932160 | tf_op jit(solution)/shard_map/all_gather | solution.py:214
  145.6 156.9 %all-reduce.4.cloned.1.call-start = ((), (), s32[]{:S(2)}) async-start(), calls=%async_computation.5 | async-start | bytes 4194304
  185.7 4.7 %copy-start.5 = (bf16[512,1024]{1,0:T(8,128)(2,1)S(1)}, bf16[512,1024]{1,0:T(8,128)(2,1)}, u32[]{:S(2)}) copy-start(bf16[512,1024]{1,0:T(8,128)(2,1)} %squeeze.26) | copy-start | bytes 3145732
  196.2 4.3 %copy-start.9 = (u32[32]{0:T(128)S(1)}, u32[32]{0:T(128)}, u32[]{:S(2)}) copy-start(u32[32]{0:T(128)} %constant.11) | copy-start | bytes 388
  196.2 5.6 %copy-start = (bf16[3,512,1024]{2,1,0:T(8,128)(2,1)S(1)}, bf16[3,512,1024]{2,1,0:T(8,128)(2,1)}, u32[]{:S(2)}) copy-start(bf16[3,512,1024]{2,1,0:T(8,128)(2,1)} %all-gather.5.cloned.1.call-done.g) | copy-start | bytes 9437188
  201.8 1.6 copy-start.1
Sparse Core Ops, SparseCore 0:
  10.8 51.9 all-gather.2
  145.7 28.1 all-gather.4
  200.7 101.8 all-reduce.3

commit v2 on v1

--- a/solution.py
+++ b/solution.py
@@ -172,6 +172,364 @@
     )(feat, short_filter.reshape(9, channels), taps, taps[:, ::-1], skip_gain[None], upstream)
 
 
+def remote(src, dst, send, recv, where):
+    return pltpu.make_async_remote_copy(
+        src_ref=src, dst_ref=dst, send_sem=send, recv_sem=recv, device_id=where, device_id_type=MESH)
+
+
+class Place:
+    def __init__(self, levels):
+        self.f = lax.axis_index("fsdp")
+        self.t = lax.axis_index("tp")
+        self.levels = levels
+        self.z, self.y = self.t // 2, lax.rem(self.t, 2)
+        self.x, self.core = self.f // 2, lax.rem(self.f, 2)
+        self.pair = (self.f, 2 * self.z + 1 - self.y)
+        self.up = (self.f, 2 * lax.rem(self.z + 1, levels) + self.y)
+        self.down = (self.f, 2 * lax.rem(self.z + levels - 1, levels) + self.y)
+        self.twin = (2 * self.x + 1 - self.core, self.t)
+        self.across = (2 * (1 - self.x) + self.core, self.t)
+
+    def greet(self):
+        barrier = pltpu.get_barrier_semaphore()
+        peers = (self.pair, self.up, self.down, self.twin, self.across)
+        for peer in peers:
+            pl.semaphore_signal(barrier, inc=1, device_id=peer, device_id_type=MESH)
+        pl.semaphore_wait(barrier, len(peers))
+
+
+def features_kernel(
+    levels, cuts, x, w, gath, feat,
+    wv, rows, mine, to_twin, from_twin, to_far, from_far,
+    w_sem, got, pair_sem, up_sem, down_sem, twin_send, twin_got, far_send, far_got,
+):
+    at = Place(levels)
+    blocks, own, depth = x.shape
+    tokens, channels = gath.shape[1], w.shape[2]
+    span = tokens + HALO
+    part = depth // cuts
+    loads = [pltpu.make_async_copy(w.at[i], wv.at[i], w_sem.at[i]) for i in range(3)]
+    for load in loads:
+        load.start()
+    gath[:, pl.ds(pl.multiple_of(at.t * own, own), own), :] = x[...]
+    at.greet()
+
+    def shard(t, h):
+        return gath.at[:, pl.ds(pl.multiple_of(t * own, own), own), pl.ds(h * part, part)]
+
+    def push(t, h, send, where):
+        return remote(shard(t, h), shard(t, h), send, got.at[t, h], where)
+
+    def source(k):
+        return 2 * (at.z - k) + at.y
+
+    def upward(k, h):
+        return push(source(k), h, up_sem.at[k, h], at.up)
+
+    def downward(k, h):
+        return push(source(-k), h, down_sem.at[k, h], at.down)
+
+    def sideways(k, h):
+        return push(source(k), h, pair_sem.at[k + levels, h], at.pair)
+
+    can_up, can_down = at.z < levels - 1, at.z > 0
+    for h in range(cuts):
+        @pl.when(can_up)
+        def _():
+            upward(0, h).start()
+
+        @pl.when(can_down)
+        def _():
+            downward(0, h).start()
+
+        sideways(0, h).start()
+    for k in range(1, levels):
+        for h in range(cuts):
+            @pl.when(at.z >= k)
+            def _():
+                sideways(k, h).wait_recv()
+
+                @pl.when(can_up)
+                def _():
+                    upward(k, h).start()
+
+                sideways(k, h).start()
+
+            @pl.when(at.z + k < levels)
+            def _():
+                sideways(-k, h).wait_recv()
+
+                @pl.when(can_down)
+                def _():
+                    downward(k, h).start()
+
+                sideways(-k, h).start()
+    for z in range(levels):
+        for h in range(cuts):
+            push(2 * z + 1 - at.y, h, pair_sem.at[0, 0], at.pair).wait_recv()
+
+    tile = min(256, channels)
+    for phase in range(2):
+        side = 1 - at.x if phase == 0 else at.x
+        for c in range(2):
+            block = 2 * side + c
+            before = gath[jnp.maximum(block - 1, 0), pl.ds(tokens - HALO, HALO), :]
+            rows[pl.ds(c * span, HALO), :] = jnp.where(block > 0, before, jnp.zeros_like(before))
+            rows[pl.ds(c * span + HALO, tokens), :] = gath[block]
+        for i in range(3):
+            if phase == 0:
+                loads[i].wait()
+
+            def step(n, _):
+                cols = pl.ds(pl.multiple_of(n * tile, tile), tile)
+                both = jnp.dot(rows[...], wv[i, :, cols], preferred_element_type=F32)
+                low, high = both[:span], both[span:]
+                mine[i, :, cols] = jnp.where(at.core == 0, low, high)
+                to_twin[phase, i, :, cols] = jnp.where(at.core == 0, high, low).astype(BF16)
+                return 0
+
+            lax.fori_loop(0, channels // tile, step, 0)
+            swap = remote(
+                to_twin.at[phase, i], from_twin.at[phase, i], twin_send.at[phase, i], twin_got.at[phase, i], at.twin)
+            swap.start()
+            if phase == 0:
+                swap.wait_recv()
+                to_far[i] = (mine[i] + from_twin[0, i].astype(F32)).astype(BF16)
+                remote(to_far.at[i], from_far.at[i], far_send.at[i], far_got.at[i], at.across).start()
+    for i in range(3):
+        far = remote(to_far.at[i], from_far.at[i], far_send.at[i], far_got.at[i], at.across)
+        swap = remote(to_twin.at[1, i], from_twin.at[1, i], twin_send.at[1, i], twin_got.at[1, i], at.twin)
+        swap.wait_recv()
+        far.wait_recv()
+        feat[i] = (mine[i] + from_twin[1, i].astype(F32) + from_far[i].astype(F32)).astype(BF16)
+
+    for i in range(3):
+        remote(to_far.at[i], from_far.at[i], far_send.at[i], far_got.at[i], at.across).wait_send()
+        for phase in range(2):
+            remote(
+                to_twin.at[phase, i], from_twin.at[phase, i], twin_send.at[phase, i], twin_got.at[phase, i], at.twin
+            ).wait_send()
+    for h in range(cuts):
+        for k in range(levels):
+            @pl.when(jnp.logical_and(can_up, at.z >= k))
+            def _():
+                upward(k, h).wait_send()
+
+            @pl.when(jnp.logical_and(can_down, at.z + k < levels))
+            def _():
+                downward(k, h).wait_send()
+
+            @pl.when(at.z >= k)
+            def _():
+                sideways(k, h).wait_send()
+
+            if k > 0:
+                @pl.when(at.z + k < levels)
+                def _():
+                    sideways(-k, h).wait_send()
+
+
+def gather_features(x, w, ways):
+    blocks, own, depth = x.shape
+    channels = w.shape[2]
+    levels, cuts = ways // 2, 2
+    tokens = own * ways
+    span = tokens + HALO
+    half = pltpu.VMEM((3, span, channels), BF16)
+    twice = pltpu.VMEM((2, 3, span, channels), BF16)
+    dma = pltpu.SemaphoreType.DMA
+    return pl.pallas_call(
+        functools.partial(features_kernel, levels, cuts),
+        out_shape=(
+            jax.ShapeDtypeStruct((blocks, tokens, depth), BF16), jax.ShapeDtypeStruct((3, span, channels), BF16)),
+        in_specs=[VMEM, pl.BlockSpec(memory_space=pl.ANY)],
+        out_specs=(VMEM, VMEM),
+        scratch_shapes=[
+            pltpu.VMEM(w.shape, BF16), pltpu.VMEM((2 * span, depth), BF16),
+            pltpu.VMEM((3, span, channels), F32), twice, twice, half, half,
+            dma((3,)), dma((ways, cuts)), dma((2 * levels, cuts)), dma((levels, cuts)), dma((levels, cuts)),
+            dma((2, 3)), dma((2, 3)), dma((3,)), dma((3,)),
+        ],
+        compiler_params=pltpu.CompilerParams(collective_id=0, has_side_effects=True, vmem_limit_bytes=48 * 2**20),
+    )(x, w)
+
+
+def input_grad_kernel(
+    levels, g, w, grads, out,
+    wv, partial, side_in, up_in, down_in, staged, total,
+    w_sem, twin_send, twin_got, far_send, far_got, pass_send, pass_got,
+    side_send, side_got, line_send, up_got, down_got,
+):
+    at = Place(levels)
+    blocks, own, depth = out.shape
+    channels, tokens = g.shape[2], g.shape[1]
+    loads = [pltpu.make_async_copy(w.at[i], wv.at[i], w_sem.at[i]) for i in range(3)]
+    for load in loads:
+        load.start()
+    for i in range(3):
+        grads[i, at.f] = g[i]
+    at.greet()
+    there = 2 * (1 - at.x) + at.core
+
+    def to_far(i):
+        return remote(grads.at[i, at.f], grads.at[i, at.f], far_send.at[i], far_got.at[i], at.across)
+
+    def to_twin(i):
+        return remote(grads.at[i, at.f], grads.at[i, at.f], twin_send.at[i], twin_got.at[i], at.twin)
+
+    def passed(i):
+        return remote(grads.at[i, there], grads.at[i, there], pass_send.at[i], pass_got.at[i], at.twin)
+
+    for i in range(3):
+        to_far(i).start()
+        to_twin(i).start()
+
+    tile = min(256, depth)
+
+    def multiply(half):
+        side = at.x if half == 0 else 1 - at.x
+
+        def step(n, _):
+            cols = pl.ds(pl.multiple_of(n * tile, tile), tile)
+            acc = None
+            for i in range(3):
+                pair = grads[i, pl.ds(2 * side, 2)].reshape(2 * tokens, channels)
+                term = lax.dot_general(pair, wv[i, cols, :], (((1,), (1,)), ((), ())), preferred_element_type=F32)
+                acc = term if acc is None else acc + term
+            partial[half, :, :, cols] = acc.astype(BF16).reshape(2, tokens, tile)
+            return 0
+
+        lax.fori_loop(0, depth // tile, step, 0)
+
+    def piece(half, t):
+        return partial.at[half, :, pl.ds(pl.multiple_of(t * own, own), own)]
+
+    def sideways(half, z):
+        return remote(
+            piece(half, 2 * z + 1 - at.y), side_in.at[half, z], side_send.at[half, z], side_got.at[half, z], at.pair)
+
+    def upward(half, z):
+        return remote(staged.at[half, z], up_in.at[half, z], line_send.at[half, z], up_got.at[half, z], at.up)
+
+    def downward(half, z):
+        return remote(staged.at[half, z], down_in.at[half, z], line_send.at[half, z], down_got.at[half, z], at.down)
+
+    def own_sum(half, z):
+        sideways(half, z).wait_recv()
+        return piece(half, 2 * z + at.y)[...].astype(F32) + side_in[half, z].astype(F32)
+
+    def start_side(half):
+        for k in range(levels - 1, 0, -1):
+            @pl.when(at.z + k < levels)
+            def _():
+                sideways(half, at.z + k).start()
+
+            @pl.when(at.z >= k)
+            def _():
+                sideways(half, at.z - k).start()
+
+        sideways(half, at.z).start()
+
+    def line(half, k):
+        @pl.when(at.z + k < levels)
+        def _():
+            z = at.z + k
+            staged[half, z] = own_sum(half, z).astype(BF16)
+
+            @pl.when(at.z > 0)
+            def _():
+                upward(half, z).wait_recv()
+                staged[half, z] = (staged[half, z].astype(F32) + up_in[half, z].astype(F32)).astype(BF16)
+
+            upward(half, z).start()
+
+        @pl.when(at.z >= k)
+        def _():
+            z = at.z - k
+            staged[half, z] = own_sum(half, z).astype(BF16)
+
+            @pl.when(at.z < levels - 1)
+            def _():
+                downward(half, z).wait_recv()
+                staged[half, z] = (staged[half, z].astype(F32) + down_in[half, z].astype(F32)).astype(BF16)
+
+            downward(half, z).start()
+
+    def finish(half):
+        z = at.z
+        side = at.x if half == 0 else 1 - at.x
+        total[...] = own_sum(half, z)
+
+        @pl.when(z > 0)
+        def _():
+            upward(half, z).wait_recv()
+            total[...] += up_in[half, z].astype(F32)
+
+        @pl.when(z < levels - 1)
+        def _():
+            downward(half, z).wait_recv()
+            total[...] += down_in[half, z].astype(F32)
+
+        out[pl.ds(2 * side, 2)] = total[...].astype(BF16)
+
+    for i in range(3):
+        loads[i].wait()
+        to_twin(i).wait_recv()
+    multiply(0)
+    start_side(0)
+    for i in range(3):
+        if i < levels - 1:
+            line(0, levels - 1 - i)
+        to_far(i).wait_recv()
+        passed(i).start()
+    for k in range(levels - 4, 0, -1):
+        line(0, k)
+    for i in range(3):
+        passed(i).wait_recv()
+    multiply(1)
+    start_side(1)
+    finish(0)
+    for k in range(levels - 1, 0, -1):
+        line(1, k)
+    finish(1)
+
+    for i in range(3):
+        to_far(i).wait_send()
+        to_twin(i).wait_send()
+        passed(i).wait_send()
+    for half in range(2):
+        for z in range(levels):
+            sideways(half, z).wait_send()
+
+            @pl.when(z != at.z)
+            def _():
+                upward(half, z).wait_send()
+
+
+def input_product(g, w, ways):
+    blocks, tokens, channels = 4, g.shape[1], g.shape[2]
+    depth = w.shape[1]
+    levels, own = ways // 2, tokens // ways
+    pieces = pltpu.VMEM((2, levels, 2, own, depth), BF16)
+    dma = pltpu.SemaphoreType.DMA
+    lines = dma((2, levels))
+    return pl.pallas_call(
+        functools.partial(input_grad_kernel, levels),
+        out_shape=(
+            jax.ShapeDtypeStruct((3, blocks, tokens, channels), BF16),
+            jax.ShapeDtypeStruct((blocks, own, depth), BF16)),
+        in_specs=[VMEM, pl.BlockSpec(memory_space=pl.ANY)],
+        out_specs=(VMEM, VMEM),
+        scratch_shapes=[
+            pltpu.VMEM(w.shape, BF16), pltpu.VMEM((2, 2, tokens, depth), BF16), pieces, pieces, pieces, pieces,
+            pltpu.VMEM((2, own, depth), F32),
+            dma((3,)), dma((3,)), dma((3,)), dma((3,)), dma((3,)), dma((3,)), dma((3,)),
+            lines, lines, lines, lines, lines,
+        ],
+        compiler_params=pltpu.CompilerParams(collective_id=2, has_side_effects=True, vmem_limit_bytes=48 * 2**20),
+    )(g, w)
+
+
 def weight_kernel(x, g, out):
     out[...] = lax.dot_general(x[...], g[...], (((0,), (0,)), ((), ())), preferred_element_type=F32).astype(BF16)
 
@@ -195,7 +553,7 @@
     )(x, grads)
 
 
-def shards(inputs, featurizer, short_filter, long_filter, decay_rate, skip_gain, output_grad):
+def shards_general(inputs, featurizer, short_filter, long_filter, decay_rate, skip_gain, output_grad):
     weights = featurizer.transpose(1, 0, 2)
     gathered = lax.all_gather(inputs.transpose(1, 0, 2), "tp", axis=1, tiled=True)
     blocks, tokens, depth = gathered.shape
@@ -221,6 +579,22 @@
     input_grad = lax.psum_scatter(
         part.astype(BF16).reshape(tokens, blocks, depth), "tp", scatter_dimension=0, tiled=True)
     return out.reshape(output_grad.shape), input_grad, weight_grad.transpose(1, 0, 2)
+
+
+def shards(inputs, featurizer, short_filter, long_filter, decay_rate, skip_gain, output_grad):
+    ways = lax.axis_size("tp")
+    if inputs.shape[0] % 16 or lax.axis_size("fsdp") != 4 or ways % 4:
+        return shards_general(inputs, featurizer, short_filter, long_filter, decay_rate, skip_gain, output_grad)
+    weights = featurizer.transpose(1, 0, 2)
+    gathered, feats = gather_features(inputs.transpose(1, 0, 2), weights, ways)
+    blocks, tokens, depth = gathered.shape
+    channels = weights.shape[2]
+    out, own_grad = hyena(
+        feats, short_filter, long_filter, decay_rate, skip_gain, output_grad.reshape(tokens, channels))
+    grads, input_grad = input_product(own_grad, weights, ways)
+    weight_grad = weight_product(
+        gathered.reshape(blocks * tokens, depth), grads.reshape(3, blocks * tokens, channels))
+    return out.reshape(output_grad.shape), input_grad.transpose(1, 0, 2), weight_grad.transpose(1, 0, 2)
 
 
 def solution(mesh):

time: 312 us -> 130 us (0.42)
  waiting for transfers between devices: 204 us -> 0 us
  Pallas kernels: 23.9 us -> 124 us
  matrix products: 34.1 us -> 0 us
  local copies, waits for them, and re-layouts: 18.9 us -> 3.62 us
  between operations: 14.7 us -> 0.7 us
  starting transfers between devices: 11.7 us -> 0 us
    pallas_call x0 -> x2, Pallas kernels: none -> 99.9 us  [the longest x1 53.6 us: gather_features(): pl.pallas_call(functools.partial(features_kernel, levels, cuts), out_shap...]
    unnamed x4 -> x0, waiting for transfers between devices: 88.1 us -> none
    all_gather x2 -> x0, waiting for transfers between devices: 81.8 us -> none  [the longest x1 53.7 us: shards(): lax.all_gather(inputs.transpose(1, 0, 2), 'tp', axis=1, tiled=True)]
    all_to_all x3 -> x0, waiting for transfers between devices: 34.4 us -> none  [shards(): lax.all_to_all(part, 'fsdp', split_axis=0, concat_axis=0, tiled=True)]
    dot_general x6 -> x0, matrix products: 34.1 us -> none  [the longest x3 19 us: shards(): jnp.dot(extended, weights[i], preferred_element_type=F32).astype(BF16)]
    all_to_all x3 -> x0, starting transfers between devices: 11.4 us -> none  [shards(): lax.all_to_all(part, 'fsdp', split_axis=0, concat_axis=0, tiled=True)]
    reshape x2 -> x0, local copies, waits for them, and re-layouts: 8.59 us -> none  [the longest x1 4.32 us: shards(): grads.reshape(3, blocks, tokens, channels).transpose(0, 2, 1, 3)]
    unnamed x24 -> x7, local copies, waits for them, and re-layouts: 6.47 us -> 2.72 us
  transfers between devices with their start and end apart: 6 -> 0, of which waited for: 6 -> 0; matrix products, arithmetic and copies ran while one was open for 4% -> 0% of each run, Pallas kernels for 4% -> 0%
where the time goes in v2:
time: 130 us
  Pallas kernels  124 us (95%)
  local copies, waits for them, and re-layouts  3.62 us (3%)
  other arithmetic  1.54 us (1%)
    pallas_call x1, Pallas kernels, gather_features(): pl.pallas_call(functools.partial(features_kernel, levels, cuts), out_shap...  53.6 us
    pallas_call x1, Pallas kernels, input_product(): pl.pallas_call(functools.partial(input_grad_kernel, levels), out_shape=(j...  46.3 us
    pallas_call x1, Pallas kernels, hyena(): pl.pallas_call(functools.partial(hyena_kernel, lax.axis_size('fsdp'), wid...  12.8 us
    pallas_call x1, Pallas kernels, weight_product(): pl.pallas_call(weight_kernel, grid=(depth // step, 3), out_shape=jax.Shap...  11.2 us
    unnamed x7, local copies, waits for them, and re-layouts  2.72 us

profile of v2, /device:TPU:0, one launch (start us, length us, event | category | flops | bytes accessed | tf_op | source)
XLA Modules:
  0.0 129.7 jit_solution(1995063734934748970)
XLA Ops:
  0.6 0.0 copy-start
  0.6 0.0 copy-start.1
  0.7 0.7 neg.4
  1.4 0.8 exponential_multiply_fusion.taps
  2.2 0.1 rev.3.taps_back
  2.3 0.8 reshape.27.short
  3.1 1.1 copy.13
  4.2 53.6 %shard_map.94 = (bf16[4,128,2048]{2,1,0:T(8,128)(2,1)S(1)}, bf16[3,144,1024]{2,1,0:T(8,128)(2,1)S(1)}) custom-call(bf16[4,16,2048]{2,1,0:T(8,128)(2,1)S(1)} %bitcast.11, bf16[3,2048,1024]{2,1,0:T(8,128)(2,1)} %bitcast.18), custom_call_target="tpu_custom_call" | custom-call | tf_op jit(solution)/shard_map/pallas_call | solution.py:341
  57.8 0.0 copy-done
  57.8 0.0 copy-done.1
  57.8 12.8 %shard_map.95 = (bf16[128,1024]{1,0:T(8,128)(2,1)S(1)}, bf16[3,128,1024]{2,1,0:T(8,128)(2,1)S(1)}) custom-call(bf16[3,144,1024]{2,1,0:T(8,128)(2,1)S(1)} %get-tuple-element.9.feat, f32[9,1024]{1,0:T(8,128)S(1)} %reshape.27.short, f32[64,128]{1,0:T(8,128)S(1)} %exponential_multiply_fusion.taps, f32[64,128]{1,0:T(8,128)S(1)} %rev.3.taps_back, ...), custom_call_target="tpu_custom_call" | custom-call | tf_op jit(solution)/shard_map/pallas_call | solution.py:161
  70.6 46.3 %shard_map.96 = (bf16[3,4,128,1024]{3,2,1,0:T(8,128)(2,1)S(1)}, bf16[4,16,2048]{2,1,0:T(8,128)(2,1)S(1)}) custom-call(bf16[3,128,1024]{2,1,0:T(8,128)(2,1)S(1)} %get-tuple-element.11.g, bf16[3,2048,1024]{2,1,0:T(8,128)(2,1)} %bitcast.19), custom_call_target="tpu_custom_call" | custom-call | tf_op jit(solution)/shard_map/pallas_call | solution.py:516
  116.9 0.9 copy.11
  117.8 11.2 %shard_map.97 = bf16[3,2048,1024]{2,1,0:T(8,128)(2,1)} custom-call(bf16[512,2048]{1,0:T(8,128)(2,1)S(1)} %bitcast.17, bf16[3,512,1024]{2,1,0:T(8,128)(2,1)S(1)} %bitcast.16), custom_call_target="tpu_custom_call" | custom-call | flops 6442450944 | bytes 12582912 | tf_op jit(solution)/shard_map/pallas_call | solution.py:541
  129.0 0.7 copy.15
  (1 shorter events, 0.0 us)
Async XLA Ops:
  0.6 57.2 %copy-start = (bf16[128,1,1024]{2,0,1:T(8,128)(2,1)S(1)}, bf16[128,1,1024]{2,0,1:T(8,128)(2,1)}, u32[]{:S(2)}) copy-start(bf16[128,1,1024]{2,0,1:T(8,128)(2,1)} %param.13) | copy-start | bytes 786436
  0.6 57.2 %copy-start.1 = (f32[1024]{0:T(1024)S(1)}, f32[1024]{0:T(1024)}, u32[]{:S(2)}) copy-start(f32[1024]{0:T(1024)} %param.12) | copy-start | bytes 12292

commit v3 on v2

--- a/solution.py
+++ b/solution.py
@@ -190,6 +190,13 @@
         self.twin = (2 * self.x + 1 - self.core, self.t)
         self.across = (2 * (1 - self.x) + self.core, self.t)
 
+    def nearest(self, step):
+        levels, z = self.levels, self.z
+        paired = jnp.minimum(z, levels - 1 - z)
+        near = (step + 1) // 2 * (1 if step % 2 == 0 else -1)
+        far = (step - paired) * jnp.where(z < levels - 1 - z, 1, -1)
+        return z + jnp.where(step <= 2 * paired, near, far)
+
     def greet(self):
         barrier = pltpu.get_barrier_semaphore()
         peers = (self.pair, self.up, self.down, self.twin, self.across)
@@ -199,15 +206,15 @@
 
 
 def features_kernel(
-    levels, cuts, x, w, gath, feat,
-    wv, rows, mine, to_twin, from_twin, to_far, from_far,
-    w_sem, got, pair_sem, up_sem, down_sem, twin_send, twin_got, far_send, far_got,
+    levels, cuts, x, w, turned, feat,
+    gath, wv, result, mine, total, to_twin, from_twin, to_far, from_far,
+    w_sem, got, pair_sem, up_sem, down_sem, twin_send, twin_got, far_send, far_got, edge_send, edge_got,
 ):
     at = Place(levels)
     blocks, own, depth = x.shape
     tokens, channels = gath.shape[1], w.shape[2]
-    span = tokens + HALO
     part = depth // cuts
+    both = 2 * own
     loads = [pltpu.make_async_copy(w.at[i], wv.at[i], w_sem.at[i]) for i in range(3)]
     for load in loads:
         load.start()
@@ -243,6 +250,72 @@
             downward(0, h).start()
 
         sideways(0, h).start()
+
+    tile = min(256, channels)
+    main, edge = pl.ds(0, both), pl.ds(both, HALO)
+    last = levels - 1
+
+    def swap(n, i):
+        return remote(to_twin.at[n, i], from_twin.at[n, i], twin_send.at[n, i], twin_got.at[n, i], at.twin)
+
+    def far(i, z):
+        spot = pl.ds(pl.multiple_of(HALO + z * both, HALO), both)
+        return remote(to_far.at[i, spot], from_far.at[i, spot], far_send.at[i, z], far_got.at[i, z], at.across)
+
+    def far_edge(i):
+        spot = pl.ds(0, HALO)
+        return remote(to_far.at[i, spot], from_far.at[i, spot], edge_send.at[i], edge_got.at[i], at.across)
+
+    def passed_on(n, i):
+        z = at.nearest(n)
+        spot = pl.ds(pl.multiple_of(HALO + z * both, HALO), both)
+        slot = (3 * n + i) % 2
+        swap(n, i).wait_recv()
+        to_far[i, spot] = (mine[slot, 0, main] + from_twin[n, i, 0, main].astype(F32)).astype(BF16)
+        far(i, z).start()
+        total[i, spot] = mine[slot, 1, main] + from_twin[n, i, 1, main].astype(F32)
+
+        @pl.when(z == last)
+        def _():
+            spot = pl.ds(0, HALO)
+            to_far[i, spot] = (mine[slot, 0, edge] + from_twin[n, i, 0, edge].astype(F32)).astype(BF16)
+            far_edge(i).start()
+            total[i, spot] = mine[slot, 1, edge] + from_twin[n, i, 1, edge].astype(F32)
+
+    def group(n):
+        z = at.nearest(n)
+        for h in range(cuts):
+            push(2 * z + 1 - at.y, h, pair_sem.at[0, 0], at.pair).wait_recv()
+        spot = pl.ds(pl.multiple_of(z * both, both), both)
+        for i in range(3):
+            if n == 0:
+                loads[i].wait()
+
+            def step(m, _):
+                cols = pl.ds(pl.multiple_of(m * tile, tile), tile)
+                lines = gath[:, spot, :].reshape(blocks * both, depth)
+                term = jnp.dot(lines, wv[i, :, cols], preferred_element_type=F32)
+                result[:, :, cols] = term.reshape(blocks, both, tile)
+                return 0
+
+            lax.fori_loop(0, channels // tile, step, 0)
+            slot = (3 * n + i) % 2
+            for phase in range(2):
+                side = 1 - at.x if phase == 0 else at.x
+                for other in range(2):
+                    block = 2 * side + (1 - at.core if other else at.core)
+                    before = result[jnp.maximum(block - 1, 0), pl.ds(both - HALO, HALO), :]
+                    before = jnp.where(block > 0, before, jnp.zeros_like(before))
+                    if other:
+                        to_twin[n, i, phase, main] = result[block].astype(BF16)
+                        to_twin[n, i, phase, edge] = before.astype(BF16)
+                    else:
+                        mine[slot, phase, main] = result[block]
+                        mine[slot, phase, edge] = before
+            swap(n, i).start()
+            if n + i > 0:
+                passed_on(n if i > 0 else n - 1, i - 1 if i > 0 else 2)
+
     for k in range(1, levels):
         for h in range(cuts):
             @pl.when(at.z >= k)
@@ -264,51 +337,23 @@
                     downward(k, h).start()
 
                 sideways(-k, h).start()
-    for z in range(levels):
-        for h in range(cuts):
-            push(2 * z + 1 - at.y, h, pair_sem.at[0, 0], at.pair).wait_recv()
-
-    tile = min(256, channels)
-    for phase in range(2):
-        side = 1 - at.x if phase == 0 else at.x
-        for c in range(2):
-            block = 2 * side + c
-            before = gath[jnp.maximum(block - 1, 0), pl.ds(tokens - HALO, HALO), :]
-            rows[pl.ds(c * span, HALO), :] = jnp.where(block > 0, before, jnp.zeros_like(before))
-            rows[pl.ds(c * span + HALO, tokens), :] = gath[block]
-        for i in range(3):
-            if phase == 0:
-                loads[i].wait()
-
-            def step(n, _):
-                cols = pl.ds(pl.multiple_of(n * tile, tile), tile)
-                both = jnp.dot(rows[...], wv[i, :, cols], preferred_element_type=F32)
-                low, high = both[:span], both[span:]
-                mine[i, :, cols] = jnp.where(at.core == 0, low, high)
-                to_twin[phase, i, :, cols] = jnp.where(at.core == 0, high, low).astype(BF16)
-                return 0
-
-            lax.fori_loop(0, channels // tile, step, 0)
-            swap = remote(
-                to_twin.at[phase, i], from_twin.at[phase, i], twin_send.at[phase, i], twin_got.at[phase, i], at.twin)
-            swap.start()
-            if phase == 0:
-                swap.wait_recv()
-                to_far[i] = (mine[i] + from_twin[0, i].astype(F32)).astype(BF16)
-                remote(to_far.at[i], from_far.at[i], far_send.at[i], far_got.at[i], at.across).start()
-    for i in range(3):
-        far = remote(to_far.at[i], from_far.at[i], far_send.at[i], far_got.at[i], at.across)
-        swap = remote(to_twin.at[1, i], from_twin.at[1, i], twin_send.at[1, i], twin_got.at[1, i], at.twin)
-        swap.wait_recv()
-        far.wait_recv()
-        feat[i] = (mine[i] + from_twin[1, i].astype(F32) + from_far[i].astype(F32)).astype(BF16)
-
-    for i in range(3):
-        remote(to_far.at[i], from_far.at[i], far_send.at[i], far_got.at[i], at.across).wait_send()
-        for phase in range(2):
-            remote(
-                to_twin.at[phase, i], from_twin.at[phase, i], twin_send.at[phase, i], twin_got.at[phase, i], at.twin
-            ).wait_send()
+        group(k - 1)
+    group(levels - 1)
+    passed_on(levels - 1, 2)
+    for n in range(depth // tile):
+        cols = pl.ds(n * tile, tile)
+        turned[cols, :] = gath[:, :, cols].reshape(blocks * tokens, tile).T
+    for i in range(3):
+        for z in range(levels):
+            far(i, z).wait_recv()
+        far_edge(i).wait_recv()
+        feat[i] = (total[i] + from_far[i].astype(F32)).astype(BF16)
+
+    for i in range(3):
+        for n in range(levels):
+            far(i, n).wait_send()
+            swap(n, i).wait_send()
+        far_edge(i).wait_send()
     for h in range(cuts):
         for k in range(levels):
             @pl.when(jnp.logical_and(can_up, at.z >= k))
@@ -336,19 +381,20 @@
     tokens = own * ways
     span = tokens + HALO
     half = pltpu.VMEM((3, span, channels), BF16)
-    twice = pltpu.VMEM((2, 3, span, channels), BF16)
+    swaps = pltpu.VMEM((levels, 3, 2, 2 * own + HALO, channels), BF16)
     dma = pltpu.SemaphoreType.DMA
     return pl.pallas_call(
         functools.partial(features_kernel, levels, cuts),
         out_shape=(
-            jax.ShapeDtypeStruct((blocks, tokens, depth), BF16), jax.ShapeDtypeStruct((3, span, channels), BF16)),
+            jax.ShapeDtypeStruct((depth, blocks * tokens), BF16), jax.ShapeDtypeStruct((3, span, channels), BF16)),
         in_specs=[VMEM, pl.BlockSpec(memory_space=pl.ANY)],
         out_specs=(VMEM, VMEM),
         scratch_shapes=[
-            pltpu.VMEM(w.shape, BF16), pltpu.VMEM((2 * span, depth), BF16),
-            pltpu.VMEM((3, span, channels), F32), twice, twice, half, half,
+            pltpu.VMEM((blocks, tokens, depth), BF16), pltpu.VMEM(w.shape, BF16),
+            pltpu.VMEM((blocks, 2 * own, channels), F32), pltpu.VMEM((2, 2, 2 * own + HALO, channels), F32),
+            pltpu.VMEM((3, span, channels), F32), swaps, swaps, half, half,
             dma((3,)), dma((ways, cuts)), dma((2 * levels, cuts)), dma((levels, cuts)), dma((levels, cuts)),
-            dma((2, 3)), dma((2, 3)), dma((3,)), dma((3,)),
+            dma((levels, 3)), dma((levels, 3)), dma((3, levels)), dma((3, levels)), dma((3,)), dma((3,)),
         ],
         compiler_params=pltpu.CompilerParams(collective_id=0, has_side_effects=True, vmem_limit_bytes=48 * 2**20),
     )(x, w)
@@ -370,33 +416,42 @@
         grads[i, at.f] = g[i]
     at.greet()
     there = 2 * (1 - at.x) + at.core
-
-    def to_far(i):
-        return remote(grads.at[i, at.f], grads.at[i, at.f], far_send.at[i], far_got.at[i], at.across)
+    both = 2 * own
+
+    def level(step):
+        return at.nearest(levels - 1 - step)
+
+    def strip(block, z):
+        return grads.at[:, block, pl.ds(pl.multiple_of(z * both, both), both)]
+
+    def to_far(z):
+        return remote(strip(at.f, z), strip(at.f, z), far_send.at[z], far_got.at[z], at.across)
 
     def to_twin(i):
         return remote(grads.at[i, at.f], grads.at[i, at.f], twin_send.at[i], twin_got.at[i], at.twin)
 
-    def passed(i):
-        return remote(grads.at[i, there], grads.at[i, there], pass_send.at[i], pass_got.at[i], at.twin)
-
-    for i in range(3):
-        to_far(i).start()
+    def passed(z):
+        return remote(strip(there, z), strip(there, z), pass_send.at[z], pass_got.at[z], at.twin)
+
+    for step in range(levels):
+        to_far(level(step)).start()
+    for i in range(3):
         to_twin(i).start()
 
     tile = min(256, depth)
 
-    def multiply(half):
+    def multiply(half, start, count):
         side = at.x if half == 0 else 1 - at.x
+        span = pl.ds(start, count)
 
         def step(n, _):
             cols = pl.ds(pl.multiple_of(n * tile, tile), tile)
             acc = None
             for i in range(3):
-                pair = grads[i, pl.ds(2 * side, 2)].reshape(2 * tokens, channels)
-                term = lax.dot_general(pair, wv[i, cols, :], (((1,), (1,)), ((), ())), preferred_element_type=F32)
+                lines = grads[i, pl.ds(2 * side, 2), span].reshape(2 * count, channels)
+                term = lax.dot_general(lines, wv[i, cols, :], (((1,), (1,)), ((), ())), preferred_element_type=F32)
                 acc = term if acc is None else acc + term
-            partial[half, :, :, cols] = acc.astype(BF16).reshape(2, tokens, tile)
+            partial[half, :, span, cols] = acc.astype(BF16).reshape(2, count, tile)
             return 0
 
         lax.fori_loop(0, depth // tile, step, 0)
@@ -418,24 +473,11 @@
         sideways(half, z).wait_recv()
         return piece(half, 2 * z + at.y)[...].astype(F32) + side_in[half, z].astype(F32)
 
-    def start_side(half):
-        for k in range(levels - 1, 0, -1):
-            @pl.when(at.z + k < levels)
-            def _():
-                sideways(half, at.z + k).start()
-
-            @pl.when(at.z >= k)
-            def _():
-                sideways(half, at.z - k).start()
-
-        sideways(half, at.z).start()
-
-    def line(half, k):
-        @pl.when(at.z + k < levels)
+    def line(half, z):
+        staged[half, z] = own_sum(half, z).astype(BF16)
+
+        @pl.when(z > at.z)
         def _():
-            z = at.z + k
-            staged[half, z] = own_sum(half, z).astype(BF16)
-
             @pl.when(at.z > 0)
             def _():
                 upward(half, z).wait_recv()
@@ -443,11 +485,8 @@
 
             upward(half, z).start()
 
-        @pl.when(at.z >= k)
+        @pl.when(z < at.z)
         def _():
-            z = at.z - k
-            staged[half, z] = own_sum(half, z).astype(BF16)
-
             @pl.when(at.z < levels - 1)
             def _():
                 downward(half, z).wait_recv()
@@ -475,30 +514,29 @@
     for i in range(3):
         loads[i].wait()
         to_twin(i).wait_recv()
-    multiply(0)
-    start_side(0)
-    for i in range(3):
-        if i < levels - 1:
-            line(0, levels - 1 - i)
-        to_far(i).wait_recv()
-        passed(i).start()
-    for k in range(levels - 4, 0, -1):
-        line(0, k)
-    for i in range(3):
-        passed(i).wait_recv()
-    multiply(1)
-    start_side(1)
+    multiply(0, 0, tokens)
+    for step in range(levels):
+        sideways(0, level(step)).start()
+    for step in range(levels):
+        z = level(step)
+        to_far(z).wait_recv()
+        passed(z).start()
+        if step < levels - 1:
+            line(0, z)
+        passed(z).wait_recv()
+        multiply(1, pl.multiple_of(z * both, both), both)
+        sideways(1, z).start()
+        if step > 0:
+            line(1, level(step - 1))
     finish(0)
-    for k in range(levels - 1, 0, -1):
-        line(1, k)
     finish(1)
 
     for i in range(3):
-        to_far(i).wait_send()
         to_twin(i).wait_send()
-        passed(i).wait_send()
-    for half in range(2):
-        for z in range(levels):
+    for z in range(levels):
+        to_far(z).wait_send()
+        passed(z).wait_send()
+        for half in range(2):
             sideways(half, z).wait_send()
 
             @pl.when(z != at.z)
@@ -523,7 +561,7 @@
         scratch_shapes=[
             pltpu.VMEM(w.shape, BF16), pltpu.VMEM((2, 2, tokens, depth), BF16), pieces, pieces, pieces, pieces,
             pltpu.VMEM((2, own, depth), F32),
-            dma((3,)), dma((3,)), dma((3,)), dma((3,)), dma((3,)), dma((3,)), dma((3,)),
+            dma((3,)), dma((3,)), dma((3,)), dma((levels,)), dma((levels,)), dma((levels,)), dma((levels,)),
             lines, lines, lines, lines, lines,
         ],
         compiler_params=pltpu.CompilerParams(collective_id=2, has_side_effects=True, vmem_limit_bytes=48 * 2**20),
@@ -531,11 +569,11 @@
 
 
 def weight_kernel(x, g, out):
-    out[...] = lax.dot_general(x[...], g[...], (((0,), (0,)), ((), ())), preferred_element_type=F32).astype(BF16)
+    out[...] = jnp.dot(x[...], g[...], preferred_element_type=F32).astype(BF16)
 
 
 def weight_product(x, grads):
-    rows, depth = x.shape
+    depth, rows = x.shape
     channels = grads.shape[2]
     step = min(512, depth)
     return pl.pallas_call(
@@ -543,7 +581,7 @@
         grid=(depth // step, 3),
         out_shape=jax.ShapeDtypeStruct((3, depth, channels), BF16),
         in_specs=[
-            pl.BlockSpec((rows, step), lambda d, i: (0, d)),
+            pl.BlockSpec((step, rows), lambda d, i: (d, 0)),
             pl.BlockSpec((None, rows, channels), lambda d, i: (i, 0, 0)),
         ],
         out_specs=pl.BlockSpec((None, step, channels), lambda d, i: (i, d, 0)),
@@ -575,7 +613,7 @@
     for i in range(3):
         term = lax.dot_general(turned[i], weights[i], (((1,), (1,)), ((), ())), preferred_element_type=F32)
         part = term if part is None else part + term
-    weight_grad = weight_product(gathered.reshape(blocks * tokens, depth), grads)
+    weight_grad = weight_product(gathered.reshape(blocks * tokens, depth).T, grads)
     input_grad = lax.psum_scatter(
         part.astype(BF16).reshape(tokens, blocks, depth), "tp", scatter_dimension=0, tiled=True)
     return out.reshape(output_grad.shape), input_grad, weight_grad.transpose(1, 0, 2)
@@ -586,14 +624,12 @@
     if inputs.shape[0] % 16 or lax.axis_size("fsdp") != 4 or ways % 4:
         return shards_general(inputs, featurizer, short_filter, long_filter, decay_rate, skip_gain, output_grad)
     weights = featurizer.transpose(1, 0, 2)
-    gathered, feats = gather_features(inputs.transpose(1, 0, 2), weights, ways)
-    blocks, tokens, depth = gathered.shape
-    channels = weights.shape[2]
+    turned, feats = gather_features(inputs.transpose(1, 0, 2), weights, ways)
+    tokens, channels = output_grad.shape[0], output_grad.shape[2]
     out, own_grad = hyena(
         feats, short_filter, long_filter, decay_rate, skip_gain, output_grad.reshape(tokens, channels))
     grads, input_grad = input_product(own_grad, weights, ways)
-    weight_grad = weight_product(
-        gathered.reshape(blocks * tokens, depth), grads.reshape(3, blocks * tokens, channels))
+    weight_grad = weight_product(turned, grads.reshape(3, turned.shape[1], channels))
     return out.reshape(output_grad.shape), input_grad.transpose(1, 0, 2), weight_grad.transpose(1, 0, 2)
 
 

time: 130 us -> 122 us (0.938)
  Pallas kernels: 124 us -> 116 us
    pallas_call x1, Pallas kernels: 53.6 us -> 43.3 us  [gather_features(): pl.pallas_call(functools.partial(features_kernel, levels, cuts), out_shap...]
    pallas_call x1, Pallas kernels: 46.3 us -> 50.1 us  [input_product(): pl.pallas_call(functools.partial(input_grad_kernel, levels), out_shape=(j...]
where the time goes in v3:
time: 122 us
  Pallas kernels  116 us (95%)
  local copies, waits for them, and re-layouts  3.62 us (3%)
  other arithmetic  1.54 us (1%)
    pallas_call x1, Pallas kernels, input_product(): pl.pallas_call(functools.partial(input_grad_kernel, levels), out_shape=(j...  50.1 us
    pallas_call x1, Pallas kernels, gather_features(): pl.pallas_call(functools.partial(features_kernel, levels, cuts), out_shap...  43.3 us
    pallas_call x1, Pallas kernels, hyena(): pl.pallas_call(functools.partial(hyena_kernel, lax.axis_size('fsdp'), wid...  11.7 us
    pallas_call x1, Pallas kernels, weight_product(): pl.pallas_call(weight_kernel, grid=(depth // step, 3), out_shape=jax.Shap...  10.8 us
    unnamed x7, local copies, waits for them, and re-layouts  2.72 us

profile of v3, /device:TPU:0, one launch (start us, length us, event | category | flops | bytes accessed | tf_op | source)
XLA Modules:
  0.0 121.8 jit_solution(5596398478228420773)
XLA Ops:
  0.6 0.0 copy-start
  0.6 0.0 copy-start.1
  0.7 0.7 neg.4
  1.4 0.8 exponential_multiply_fusion.taps
  2.2 0.1 rev.3.taps_back
  2.3 0.8 reshape.24.short
  3.1 1.1 copy.13
  4.2 43.3 %shard_map.94 = (bf16[2048,512]{1,0:T(8,128)(2,1)S(1)}, bf16[3,144,1024]{2,1,0:T(8,128)(2,1)S(1)}) custom-call(bf16[4,16,2048]{2,1,0:T(8,128)(2,1)S(1)} %bitcast.10, bf16[3,2048,1024]{2,1,0:T(8,128)(2,1)} %bitcast.16), custom_call_target="tpu_custom_call" | custom-call | tf_op jit(solution)/shard_map/pallas_call | solution.py:386
  47.5 0.0 copy-done
  47.5 0.0 copy-done.1
  47.5 11.7 %shard_map.95 = (bf16[128,1024]{1,0:T(8,128)(2,1)S(1)}, bf16[3,128,1024]{2,1,0:T(8,128)(2,1)S(1)}) custom-call(bf16[3,144,1024]{2,1,0:T(8,128)(2,1)S(1)} %get-tuple-element.9.feat, f32[9,1024]{1,0:T(8,128)S(1)} %reshape.24.short, f32[64,128]{1,0:T(8,128)S(1)} %exponential_multiply_fusion.taps, f32[64,128]{1,0:T(8,128)S(1)} %rev.3.taps_back, ...), custom_call_target="tpu_custom_call" | custom-call | tf_op jit(solution)/shard_map/pallas_call | solution.py:161
  59.2 50.1 %shard_map.96 = (bf16[3,4,128,1024]{3,2,1,0:T(8,128)(2,1)S(1)}, bf16[4,16,2048]{2,1,0:T(8,128)(2,1)S(1)}) custom-call(bf16[3,128,1024]{2,1,0:T(8,128)(2,1)S(1)} %get-tuple-element.11.g, bf16[3,2048,1024]{2,1,0:T(8,128)(2,1)} %bitcast.17), custom_call_target="tpu_custom_call" | custom-call | tf_op jit(solution)/shard_map/pallas_call | solution.py:554
  109.3 0.9 copy.11
  110.2 10.8 %shard_map.97 = bf16[3,2048,1024]{2,1,0:T(8,128)(2,1)} custom-call(bf16[2048,512]{1,0:T(8,128)(2,1)S(1)} %get-tuple-element.13.x, bf16[3,512,1024]{2,1,0:T(8,128)(2,1)S(1)} %bitcast.15), custom_call_target="tpu_custom_call" | custom-call | flops 6442450944 | bytes 12582912 | tf_op jit(solution)/shard_map/pallas_call | solution.py:579
  121.1 0.7 copy.15
  (1 shorter events, 0.0 us)
Async XLA Ops:
  0.6 46.9 %copy-start = (bf16[128,1,1024]{2,0,1:T(8,128)(2,1)S(1)}, bf16[128,1,1024]{2,0,1:T(8,128)(2,1)}, u32[]{:S(2)}) copy-start(bf16[128,1,1024]{2,0,1:T(8,128)(2,1)} %param.13) | copy-start | bytes 786436
  0.6 46.9 %copy-start.1 = (f32[1024]{0:T(1024)S(1)}, f32[1024]{0:T(1024)}, u32[]{:S(2)}) copy-start(f32[1024]{0:T(1024)} %param.12) | copy-start | bytes 12292

commit v4 on v3

--- a/solution.py
+++ b/solution.py
@@ -17,13 +17,13 @@
 
 
 def hyena_kernel(
-    blocks, width, feat, short, taps, taps_back, skip, upstream, out, grad,
-    ext_p, ext_g, query, key, value, prod, conv_grad, filt_grad, sems, head_sems,
+    blocks, width, feat, short, long, decay, skip, upstream, out, grad,
+    taps, taps_back, toeplitz, ext_p, ext_g, query, key, value, prod, conv_grad, filt_grad, sems, head_sems,
 ):
     me = lax.axis_index("fsdp")
     rest = lax.axis_index("tp")
     tokens, channels = out.shape
-    taps_count = taps.shape[1]
+    filters, taps_count = long.shape
     has_prev = me > 0
     has_next = me < blocks - 1
     prev = jnp.maximum(me - 1, 0)
@@ -39,9 +39,9 @@
         parts = []
         for i in range(3):
             f = feat[i, :, cols].astype(F32)
-            acc = short[pl.ds(i, 1), cols] * f[HALO:]
+            acc = short[0, pl.ds(i, 1), cols] * f[HALO:]
             for j in range(1, 3):
-                acc = acc + short[pl.ds(3 * j + i, 1), cols] * pltpu.roll(f, j, 0)[HALO:]
+                acc = acc + short[j, pl.ds(i, 1), cols] * pltpu.roll(f, j, 0)[HALO:]
             parts.append(acc)
         p = parts[1] * parts[2]
         cg = upstream[:, cols].astype(F32) * parts[0]
@@ -79,33 +79,52 @@
     def _():
         ext_g[pl.ds(tokens, tokens), :] = jnp.zeros((tokens, channels), BF16)
 
-    @pl.when(has_prev)
-    def _():
-        to_next.wait_recv()
-
-    @pl.when(has_next)
-    def _():
-        to_prev.wait_recv()
-
     per_tile = LANES // width
     lane = lax.broadcasted_iota(jnp.int32, (tokens, LANES), 1) // width
-
-    def mixed(rows, ext, first):
-        acc = None
-        for g in range(per_tile):
-            line = jnp.concatenate([rows[g : g + 1], jnp.zeros((1, 2 * tokens - taps_count), F32)], axis=1)
-            wide = jnp.broadcast_to(line, (tokens, 2 * tokens))
-            toeplitz = pltpu.roll(wide, first, 1, stride=1, stride_axis=0).astype(BF16)
-            part = jnp.dot(toeplitz, ext, preferred_element_type=F32)
-            acc = part if acc is None else jnp.where(lane == g, part, acc)
+    high = lax.broadcasted_iota(jnp.int32, (filters, filters), 0)
+    wide = lax.broadcasted_iota(jnp.int32, (filters, filters), 1)
+    rates = jnp.sum(jnp.where(high == wide, jnp.broadcast_to(decay[...], (filters, filters)), 0.0), 1, keepdims=True)
+    steps = lax.broadcasted_iota(jnp.int32, (filters, taps_count), 1).astype(F32)
+    taps[...] = (long[...] * jnp.exp(-rates * steps)).astype(BF16).astype(F32)
+    rise = lax.broadcasted_iota(jnp.int32, (taps_count, taps_count), 0)
+    fall = lax.broadcasted_iota(jnp.int32, (taps_count, taps_count), 1)
+    mirror = jnp.where(rise + fall == taps_count - 1, 1.0, 0.0).astype(BF16)
+    taps_back[...] = jnp.dot(taps[...].astype(BF16), mirror, preferred_element_type=F32)
+
+    def build(at, _):
+        rows = pl.ds(pl.multiple_of(at * per_tile, per_tile), per_tile)
+        for way, source, first in ((0, taps_back, 1 + tokens - taps_count), (1, taps, 0)):
+            lines = source[rows, :]
+            for g in range(per_tile):
+                line = jnp.concatenate([lines[g : g + 1], jnp.zeros((1, 2 * tokens - taps_count), F32)], axis=1)
+                spread = jnp.broadcast_to(line, (tokens, 2 * tokens))
+                spot = pl.ds(pl.multiple_of((at * per_tile + g) * tokens, tokens), tokens)
+                toeplitz[way, spot, :] = pltpu.roll(spread, first, 1, stride=1, stride_axis=0).astype(BF16)
+        return 0
+
+    lax.fori_loop(0, channels // LANES, build, 0)
+
+    @pl.when(has_prev)
+    def _():
+        to_next.wait_recv()
+
+    @pl.when(has_next)
+    def _():
+        to_prev.wait_recv()
+
+    def mixed(at, way, ext):
+        spot = pl.ds(pl.multiple_of(at * per_tile * tokens, tokens), per_tile * tokens)
+        parts = jnp.dot(toeplitz[way, spot, :], ext, preferred_element_type=F32)
+        acc = parts[:tokens]
+        for g in range(1, per_tile):
+            acc = jnp.where(lane == g, parts[g * tokens : (g + 1) * tokens], acc)
         return acc
 
     def back(at, _):
         cols = pl.ds(pl.multiple_of(at * LANES, LANES), LANES)
-        rows = pl.ds(pl.multiple_of(at * per_tile, per_tile), per_tile)
         gain = skip[:, cols]
-        conv = mixed(taps_back[rows, :], ext_p[:, cols], 1 + tokens - taps_count) + gain * prod[:, cols]
-        pg = mixed(taps[rows, :], ext_g[:, cols], 0) + gain * conv_grad[:, cols]
+        conv = mixed(at, 0, ext_p[:, cols]) + gain * prod[:, cols]
+        pg = mixed(at, 1, ext_g[:, cols]) + gain * conv_grad[:, cols]
         out[:, cols] = (query[:, cols] * conv).astype(BF16)
         own = pl.ds(0, tokens)
         filt_grad[0, own, cols] = upstream[:, cols].astype(F32) * conv
@@ -135,9 +154,9 @@
         cols = pl.ds(pl.multiple_of(at * LANES, LANES), LANES)
         for i in range(3):
             f = filt_grad[i, :, cols]
-            acc = short[pl.ds(i, 1), cols] * f[:tokens]
+            acc = short[0, pl.ds(i, 1), cols] * f[:tokens]
             for j in range(1, 3):
-                acc = acc + short[pl.ds(3 * j + i, 1), cols] * pltpu.roll(f, tokens + HEAD - j, 0)[:tokens]
+                acc = acc + short[j, pl.ds(i, 1), cols] * pltpu.roll(f, tokens + HEAD - j, 0)[:tokens]
             grad[i, :, cols] = acc.astype(BF16)
         return 0
 
@@ -155,8 +174,8 @@
 
 def hyena(feat, short_filter, long_filter, decay_rate, skip_gain, upstream):
     tokens, channels = upstream.shape
-    taps = long_filter * jnp.exp(-decay_rate[:, None] * jnp.arange(long_filter.shape[1]).astype(F32)[None, :])
-    width = channels // long_filter.shape[0]
+    filters, taps_count = long_filter.shape
+    width = channels // filters
     wide = pltpu.VMEM((tokens, channels), F32)
     return pl.pallas_call(
         functools.partial(hyena_kernel, lax.axis_size("fsdp"), width),
@@ -164,12 +183,14 @@
         in_specs=[VMEM] * 6,
         out_specs=(VMEM, VMEM),
         scratch_shapes=[
+            pltpu.VMEM((filters, taps_count), F32), pltpu.VMEM((filters, taps_count), F32),
+            pltpu.VMEM((2, filters * tokens, 2 * tokens), BF16),
             pltpu.VMEM((2 * tokens, channels), BF16), pltpu.VMEM((2 * tokens, channels), BF16),
             wide, wide, wide, wide, wide, pltpu.VMEM((3, tokens + HEAD, channels), F32),
             pltpu.SemaphoreType.DMA((4,)), pltpu.SemaphoreType.DMA((2,)),
         ],
         compiler_params=pltpu.CompilerParams(collective_id=1, has_side_effects=True, vmem_limit_bytes=40 * 2**20),
-    )(feat, short_filter.reshape(9, channels), taps, taps[:, ::-1], skip_gain[None], upstream)
+    )(feat, short_filter, long_filter, decay_rate[None], skip_gain[None], upstream)
 
 
 def remote(src, dst, send, recv, where):
@@ -440,7 +461,7 @@
 
     tile = min(256, depth)
 
-    def multiply(half, start, count):
+    def multiply(half, start, count, first, stop):
         side = at.x if half == 0 else 1 - at.x
         span = pl.ds(start, count)
 
@@ -454,14 +475,20 @@
             partial[half, :, span, cols] = acc.astype(BF16).reshape(2, count, tile)
             return 0
 
-        lax.fori_loop(0, depth // tile, step, 0)
+        lax.fori_loop(first, stop, step, 0)
+
+    tiles = depth // tile
+    cuts = min(4, tiles)
+    width = depth // cuts
 
     def piece(half, t):
         return partial.at[half, :, pl.ds(pl.multiple_of(t * own, own), own)]
 
-    def sideways(half, z):
+    def sideways(half, z, cut):
+        cols = pl.ds(cut * width, width)
         return remote(
-            piece(half, 2 * z + 1 - at.y), side_in.at[half, z], side_send.at[half, z], side_got.at[half, z], at.pair)
+            piece(half, 2 * z + 1 - at.y).at[:, :, cols], side_in.at[half, z, :, :, cols],
+            side_send.at[half, z, cut], side_got.at[half, z, cut], at.pair)
 
     def upward(half, z):
         return remote(staged.at[half, z], up_in.at[half, z], line_send.at[half, z], up_got.at[half, z], at.up)
@@ -470,7 +497,8 @@
         return remote(staged.at[half, z], down_in.at[half, z], line_send.at[half, z], down_got.at[half, z], at.down)
 
     def own_sum(half, z):
-        sideways(half, z).wait_recv()
+        for cut in range(cuts):
+            sideways(half, z, cut).wait_recv()
         return piece(half, 2 * z + at.y)[...].astype(F32) + side_in[half, z].astype(F32)
 
     def line(half, z):
@@ -514,9 +542,10 @@
     for i in range(3):
         loads[i].wait()
         to_twin(i).wait_recv()
-    multiply(0, 0, tokens)
-    for step in range(levels):
-        sideways(0, level(step)).start()
+    for cut in range(cuts):
+        multiply(0, 0, tokens, cut * tiles // cuts, (cut + 1) * tiles // cuts)
+        for step in range(levels):
+            sideways(0, level(step), cut).start()
     for step in range(levels):
         z = level(step)
         to_far(z).wait_recv()
@@ -524,8 +553,9 @@
         if step < levels - 1:
             line(0, z)
         passed(z).wait_recv()
-        multiply(1, pl.multiple_of(z * both, both), both)
-        sideways(1, z).start()
+        for cut in range(cuts):
+            multiply(1, pl.multiple_of(z * both, both), both, cut * tiles // cuts, (cut + 1) * tiles // cuts)
+            sideways(1, z, cut).start()
         if step > 0:
             line(1, level(step - 1))
     finish(0)
@@ -537,7 +567,8 @@
         to_far(z).wait_send()
         passed(z).wait_send()
         for half in range(2):
-            sideways(half, z).wait_send()
+            for cut in range(cuts):
+                sideways(half, z, cut).wait_send()
 
             @pl.when(z != at.z)
             def _():
@@ -562,7 +593,7 @@
             pltpu.VMEM(w.shape, BF16), pltpu.VMEM((2, 2, tokens, depth), BF16), pieces, pieces, pieces, pieces,
             pltpu.VMEM((2, own, depth), F32),
             dma((3,)), dma((3,)), dma((3,)), dma((levels,)), dma((levels,)), dma((levels,)), dma((levels,)),
-            lines, lines, lines, lines, lines,
+            dma((2, levels, 4)), dma((2, levels, 4)), lines, lines, lines,
         ],
         compiler_params=pltpu.CompilerParams(collective_id=2, has_side_effects=True, vmem_limit_bytes=48 * 2**20),
     )(g, w)
@@ -575,16 +606,16 @@
 def weight_product(x, grads):
     depth, rows = x.shape
     channels = grads.shape[2]
-    step = min(512, depth)
+    step = min(256, channels)
     return pl.pallas_call(
         weight_kernel,
-        grid=(depth // step, 3),
+        grid=(3, channels // step),
         out_shape=jax.ShapeDtypeStruct((3, depth, channels), BF16),
         in_specs=[
-            pl.BlockSpec((step, rows), lambda d, i: (d, 0)),
-            pl.BlockSpec((None, rows, channels), lambda d, i: (i, 0, 0)),
+            pl.BlockSpec((depth, rows), lambda i, n: (0, 0)),
+            pl.BlockSpec((None, rows, step), lambda i, n: (i, 0, n)),
         ],
-        out_specs=pl.BlockSpec((None, step, channels), lambda d, i: (i, d, 0)),
+        out_specs=pl.BlockSpec((None, depth, step), lambda i, n: (i, 0, n)),
         compiler_params=pltpu.CompilerParams(vmem_limit_bytes=40 * 2**20),
         cost_estimate=pl.CostEstimate(
             flops=6 * rows * depth * channels, bytes_accessed=2 * 3 * depth * channels, transcendentals=0),

time: 122 us -> 122 us (level)
  Pallas kernels: 116 us -> 118 us
  other arithmetic: 1.54 us -> 0 us
    pallas_call x1, Pallas kernels: 50.1 us -> 52.7 us  [input_product(): pl.pallas_call(functools.partial(input_grad_kernel, levels), out_shape=(j...]
    unnamed x7 -> x13, local copies, waits for them, and re-layouts: 2.72 us -> 2.77 us
where the time goes in v4:
time: 122 us
  Pallas kernels  118 us (97%)
  local copies, waits for them, and re-layouts  2.77 us (2%)
    pallas_call x1, Pallas kernels, input_product(): pl.pallas_call(functools.partial(input_grad_kernel, levels), out_shape=(j...  52.7 us
    pallas_call x1, Pallas kernels, gather_features(): pl.pallas_call(functools.partial(features_kernel, levels, cuts), out_shap...  43.3 us
    pallas_call x1, Pallas kernels, hyena(): pl.pallas_call(functools.partial(hyena_kernel, lax.axis_size('fsdp'), wid...  11.3 us
    pallas_call x1, Pallas kernels, weight_product(): pl.pallas_call(weight_kernel, grid=(3, channels // step), out_shape=jax.S...  11 us
    unnamed x13, local copies, waits for them, and re-layouts  2.77 us

profile of v4, /device:TPU:0, one launch (start us, length us, event | category | flops | bytes accessed | tf_op | source)
XLA Modules:
  0.0 121.9 jit_solution(13093204189190182851)
XLA Ops:
  0.6 0.0 copy-start
  0.6 0.0 copy-start.3
  0.7 0.0 copy-start.4
  0.7 0.0 copy-start.2
  0.7 0.0 copy-start.1
  0.7 1.1 copy.13
  1.8 43.3 %shard_map.94 = (bf16[2048,512]{1,0:T(8,128)(2,1)S(1)}, bf16[3,144,1024]{2,1,0:T(8,128)(2,1)S(1)}) custom-call(bf16[4,16,2048]{2,1,0:T(8,128)(2,1)S(1)} %bitcast.11, bf16[3,2048,1024]{2,1,0:T(8,128)(2,1)} %bitcast.18), custom_call_target="tpu_custom_call" | custom-call | tf_op jit(solution)/shard_map/pallas_call | solution.py:407
  45.1 0.0 copy-done
  45.1 0.0 copy-done.3
  45.1 0.0 copy-done.4
  45.2 0.0 copy-done.2
  45.2 0.0 copy-done.1
  45.2 11.3 %shard_map.95 = (bf16[128,1024]{1,0:T(8,128)(2,1)S(1)}, bf16[3,128,1024]{2,1,0:T(8,128)(2,1)S(1)}) custom-call(bf16[3,144,1024]{2,1,0:T(8,128)(2,1)S(1)} %get-tuple-element.9.feat, f32[3,3,1024]{2,1,0:T(4,128)S(1)} %copy-done.1, f32[64,128]{1,0:T(8,128)S(1)} %copy-done.2, f32[1,64]{1,0:T(1,128)S(1)} %bitcast.16, f32[1,1024]{1,0:T(1,128)S(1)} %bitcast.15, ...), custom_call_target="tpu_custom_call" | custom-call | tf_op jit(solution)/shard_map/pallas_call | solution.py:180
  56.5 52.7 %shard_map.96 = (bf16[3,4,128,1024]{3,2,1,0:T(8,128)(2,1)S(1)}, bf16[4,16,2048]{2,1,0:T(8,128)(2,1)S(1)}) custom-call(bf16[3,128,1024]{2,1,0:T(8,128)(2,1)S(1)} %get-tuple-element.11.g, bf16[3,2048,1024]{2,1,0:T(8,128)(2,1)} %bitcast.19), custom_call_target="tpu_custom_call" | custom-call | tf_op jit(solution)/shard_map/pallas_call | solution.py:585
  109.2 0.9 copy.11
  110.1 11.0 %shard_map.97 = bf16[3,2048,1024]{2,1,0:T(8,128)(2,1)} custom-call(bf16[2048,512]{1,0:T(8,128)(2,1)S(1)} %get-tuple-element.13.x, bf16[3,512,1024]{2,1,0:T(8,128)(2,1)S(1)} %bitcast.17), custom_call_target="tpu_custom_call" | custom-call | flops 6442450944 | bytes 12582912 | tf_op jit(solution)/shard_map/pallas_call | solution.py:610
  121.2 0.7 copy.15
Async XLA Ops:
  0.6 44.5 %copy-start = (bf16[128,1,1024]{2,0,1:T(8,128)(2,1)S(1)}, bf16[128,1,1024]{2,0,1:T(8,128)(2,1)}, u32[]{:S(2)}) copy-start(bf16[128,1,1024]{2,0,1:T(8,128)(2,1)} %param.13) | copy-start | bytes 786436
  0.6 44.5 %copy-start.3 = (f32[1024]{0:T(1024)S(1)}, f32[1024]{0:T(1024)}, u32[]{:S(2)}) copy-start(f32[1024]{0:T(1024)} %param.12) | copy-start | bytes 12292
  0.7 44.5 %copy-start.4 = (f32[64]{0:T(128)S(1)}, f32[64]{0:T(128)}, u32[]{:S(2)}) copy-start(f32[64]{0:T(128)} %param.11) | copy-start | bytes 772
  0.7 44.5 %copy-start.2 = (f32[64,128]{1,0:T(8,128)S(1)}, f32[64,128]{1,0:T(8,128)}, u32[]{:S(2)}) copy-start(f32[64,128]{1,0:T(8,128)} %long.1) | copy-start | bytes 98308
  0.7 44.5 %copy-start.1 = (f32[3,3,1024]{2,1,0:T(4,128)S(1)}, f32[3,3,1024]{2,1,0:T(4,128)}, u32[]{:S(2)}) copy-start(f32[3,3,1024]{2,1,0:T(4,128)} %short.1) | copy-start | bytes 110596

commit v5 on v4

--- a/solution.py
+++ b/solution.py
@@ -217,6 +217,18 @@
         near = (step + 1) // 2 * (1 if step % 2 == 0 else -1)
         far = (step - paired) * jnp.where(z < levels - 1 - z, 1, -1)
         return z + jnp.where(step <= 2 * paired, near, far)
+
+    def farthest(self, step):
+        half = self.levels // 2
+        low = self.z < half
+        if step < half:
+            return jnp.where(low, self.levels - 1 - step, step)
+        local = jnp.where(low, self.z, self.z - half)
+        back = self.levels - 1 - step
+        paired = jnp.minimum(local, half - 1 - local)
+        near = (back + 1) // 2 * (1 if back % 2 == 0 else -1)
+        far = (back - paired) * jnp.where(local < half - 1 - local, 1, -1)
+        return self.z + jnp.where(back <= 2 * paired, near, far)
 
     def greet(self):
         barrier = pltpu.get_barrier_semaphore()
@@ -440,7 +452,7 @@
     both = 2 * own
 
     def level(step):
-        return at.nearest(levels - 1 - step)
+        return at.farthest(step)
 
     def strip(block, z):
         return grads.at[:, block, pl.ds(pl.multiple_of(z * both, both), both)]
@@ -478,7 +490,7 @@
         lax.fori_loop(first, stop, step, 0)
 
     tiles = depth // tile
-    cuts = min(4, tiles)
+    cuts = 1
     width = depth // cuts
 
     def piece(half, t):
@@ -546,18 +558,23 @@
         multiply(0, 0, tokens, cut * tiles // cuts, (cut + 1) * tiles // cuts)
         for step in range(levels):
             sideways(0, level(step), cut).start()
-    for step in range(levels):
-        z = level(step)
-        to_far(z).wait_recv()
-        passed(z).start()
-        if step < levels - 1:
-            line(0, z)
-        passed(z).wait_recv()
-        for cut in range(cuts):
-            multiply(1, pl.multiple_of(z * both, both), both, cut * tiles // cuts, (cut + 1) * tiles // cuts)
-            sideways(1, z, cut).start()
-        if step > 0:
-            line(1, level(step - 1))
+    group = levels // 2
+    other = jnp.where(at.z < group, group, 0)
+    for turn in range(2):
+        first = other if turn == 0 else group - other
+        for step in range(turn * group, (turn + 1) * group):
+            z = level(step)
+            to_far(z).wait_recv()
+            passed(z).start()
+            if step < levels - 1:
+                line(0, z)
+        for step in range(turn * group, (turn + 1) * group):
+            passed(level(step)).wait_recv()
+        multiply(1, pl.multiple_of(first * both, both), group * both, 0, tiles)
+        for step in range(turn * group, (turn + 1) * group):
+            sideways(1, level(step), 0).start()
+    for step in range(levels - 1):
+        line(1, level(step))
     finish(0)
     finish(1)
 
@@ -593,7 +610,7 @@
             pltpu.VMEM(w.shape, BF16), pltpu.VMEM((2, 2, tokens, depth), BF16), pieces, pieces, pieces, pieces,
             pltpu.VMEM((2, own, depth), F32),
             dma((3,)), dma((3,)), dma((3,)), dma((levels,)), dma((levels,)), dma((levels,)), dma((levels,)),
-            dma((2, levels, 4)), dma((2, levels, 4)), lines, lines, lines,
+            dma((2, levels, 1)), dma((2, levels, 1)), lines, lines, lines,
         ],
         compiler_params=pltpu.CompilerParams(collective_id=2, has_side_effects=True, vmem_limit_bytes=48 * 2**20),
     )(g, w)

time: 122 us -> 115 us (0.943)
  Pallas kernels: 118 us -> 111 us
    pallas_call x1, Pallas kernels: 52.7 us -> 45.5 us  [input_product(): pl.pallas_call(functools.partial(input_grad_kernel, levels), out_shape=(j...]
where the time goes in v5:
time: 115 us
  Pallas kernels  111 us (97%)
  local copies, waits for them, and re-layouts  2.77 us (2%)
    pallas_call x1, Pallas kernels, input_product(): pl.pallas_call(functools.partial(input_grad_kernel, levels), out_shape=(j...  45.5 us
    pallas_call x1, Pallas kernels, gather_features(): pl.pallas_call(functools.partial(features_kernel, levels, cuts), out_shap...  43.3 us
    pallas_call x1, Pallas kernels, hyena(): pl.pallas_call(functools.partial(hyena_kernel, lax.axis_size('fsdp'), wid...  11.3 us
    pallas_call x1, Pallas kernels, weight_product(): pl.pallas_call(weight_kernel, grid=(3, channels // step), out_shape=jax.S...  11.1 us
    unnamed x13, local copies, waits for them, and re-layouts  2.77 us

profile of v5, /device:TPU:0, one launch (start us, length us, event | category | flops | bytes accessed | tf_op | source)
XLA Modules:
  0.0 114.6 jit_solution(8750132247389645473)
XLA Ops:
  0.6 0.0 copy-start
  0.6 0.0 copy-start.3
  0.7 0.0 copy-start.4
  0.7 0.0 copy-start.2
  0.7 0.0 copy-start.1
  0.7 1.1 copy.13
  1.8 43.3 %shard_map.94 = (bf16[2048,512]{1,0:T(8,128)(2,1)S(1)}, bf16[3,144,1024]{2,1,0:T(8,128)(2,1)S(1)}) custom-call(bf16[4,16,2048]{2,1,0:T(8,128)(2,1)S(1)} %bitcast.11, bf16[3,2048,1024]{2,1,0:T(8,128)(2,1)} %bitcast.18), custom_call_target="tpu_custom_call" | custom-call | tf_op jit(solution)/shard_map/pallas_call | solution.py:419
  45.1 0.0 copy-done
  45.1 0.0 copy-done.3
  45.1 0.0 copy-done.4
  45.1 0.0 copy-done.2
  45.2 0.0 copy-done.1
  45.2 11.3 %shard_map.95 = (bf16[128,1024]{1,0:T(8,128)(2,1)S(1)}, bf16[3,128,1024]{2,1,0:T(8,128)(2,1)S(1)}) custom-call(bf16[3,144,1024]{2,1,0:T(8,128)(2,1)S(1)} %get-tuple-element.9.feat, f32[3,3,1024]{2,1,0:T(4,128)S(1)} %copy-done.1, f32[64,128]{1,0:T(8,128)S(1)} %copy-done.2, f32[1,64]{1,0:T(1,128)S(1)} %bitcast.16, f32[1,1024]{1,0:T(1,128)S(1)} %bitcast.15, ...), custom_call_target="tpu_custom_call" | custom-call | tf_op jit(solution)/shard_map/pallas_call | solution.py:180
  56.5 45.5 %shard_map.96 = (bf16[3,4,128,1024]{3,2,1,0:T(8,128)(2,1)S(1)}, bf16[4,16,2048]{2,1,0:T(8,128)(2,1)S(1)}) custom-call(bf16[3,128,1024]{2,1,0:T(8,128)(2,1)S(1)} %get-tuple-element.11.g, bf16[3,2048,1024]{2,1,0:T(8,128)(2,1)} %bitcast.19), custom_call_target="tpu_custom_call" | custom-call | tf_op jit(solution)/shard_map/pallas_call | solution.py:602
  102.0 0.9 copy.11
  102.9 11.1 %shard_map.97 = bf16[3,2048,1024]{2,1,0:T(8,128)(2,1)} custom-call(bf16[2048,512]{1,0:T(8,128)(2,1)S(1)} %get-tuple-element.13.x, bf16[3,512,1024]{2,1,0:T(8,128)(2,1)S(1)} %bitcast.17), custom_call_target="tpu_custom_call" | custom-call | flops 6442450944 | bytes 12582912 | tf_op jit(solution)/shard_map/pallas_call | solution.py:627
  113.9 0.7 copy.15
Async XLA Ops:
  0.6 44.5 %copy-start = (bf16[128,1,1024]{2,0,1:T(8,128)(2,1)S(1)}, bf16[128,1,1024]{2,0,1:T(8,128)(2,1)}, u32[]{:S(2)}) copy-start(bf16[128,1,1024]{2,0,1:T(8,128)(2,1)} %param.13) | copy-start | bytes 786436
  0.6 44.5 %copy-start.3 = (f32[1024]{0:T(1024)S(1)}, f32[1024]{0:T(1024)}, u32[]{:S(2)}) copy-start(f32[1024]{0:T(1024)} %param.12) | copy-start | bytes 12292
  0.7 44.5 %copy-start.4 = (f32[64]{0:T(128)S(1)}, f32[64]{0:T(128)}, u32[]{:S(2)}) copy-start(f32[64]{0:T(128)} %param.11) | copy-start | bytes 772
  0.7 44.5 %copy-start.2 = (f32[64,128]{1,0:T(8,128)S(1)}, f32[64,128]{1,0:T(8,128)}, u32[]{:S(2)}) copy-start(f32[64,128]{1,0:T(8,128)} %long.1) | copy-start | bytes 98308
  0.7 44.5 %copy-start.1 = (f32[3,3,1024]{2,1,0:T(4,128)S(1)}, f32[3,3,1024]{2,1,0:T(4,128)}, u32[]{:S(2)}) copy-start(f32[3,3,1024]{2,1,0:T(4,128)} %short.1) | copy-start | bytes 110596
